TPU v7x, 32 devices: a whole 2x2x4 slice. The times are simulated.
32 devices in a mesh: rows: 8 (over z, x), feat: 4 (over y, core).
Axes of the slice: x: 2, y: 2, z: 4, core: 2. Of those that a mesh axis runs over, the one named last changes fastest.
Arguments:
- edge_feats: bfloat16 [8192, 256], P(('rows', 'feat')), may hold values from -6 to 6
- edge_owner: int32 [8192, 1], P(('rows', 'feat')), may hold values from 0 to 7; in each aligned block of 256 rows (0 to 255, 256 to 511, ...) at most 64 rows name the same one
- src_local: int32 [8192], P(('rows', 'feat')), may hold values from 0 to 63
- band_slot: int32 [8192], P(('rows', 'feat')), may hold values from 0 to 8
- dst_local: int32 [8192], P(('rows', 'feat')), may hold values from 0 to 7
- w_first: bfloat16 [256, 256], replicated, may hold values from -0.375 to 0.375
- w_second: bfloat16 [256, 256], replicated, may hold values from -0.375 to 0.375
- w_third: bfloat16 [256, 256], replicated, may hold values from -0.375 to 0.375
Outputs:
- density: float32 [64, 9, 128, 128], P('rows', None, 'feat')
Inputs may be any that keep to these rules, and one draw needn't show every extreme that they name: `edge_owner`: among the 256 edges of one device (aligned blocks of rows), no index of rows is named more than 64 times, a bound that some block reaches.
All inputs are finite; a program needn't handle non-finite values.
Results may differ from a plain program's by a relative error of at most 0.0014.
Values sent between devices are 32-bit elements; how exact they have to be, the bound alone decides.
A program may use at most 64 MiB of HBM per device.

v0:
```python
import math

import jax
import jax.numpy as jnp
from jax import lax
from jax.sharding import PartitionSpec as P

BLOCK = 16
TILE = 128
BAND = 9
TILE_DEV = 8


def with_halo(block, sides, width):
    for axis, dim in sides:
        count = lax.axis_size(axis)
        forward = [(i, i + 1) for i in range(count - 1)]
        forward.append((count - 1, 0))
        backward = [(target, source) for source, target in forward]
        low = lax.ppermute(
            lax.slice_in_dim(block, block.shape[dim] - width, None, axis=dim), axis, forward
        )
        high = lax.ppermute(lax.slice_in_dim(block, 0, width, axis=dim), axis, backward)
        block = jnp.concatenate([low, block, high], axis=dim)
    return block


def edge_values(edge_feats, w_first, w_second, w_third):
    hidden_one = jax.nn.silu(
        jnp.dot(edge_feats, w_first, preferred_element_type=jnp.float32)
    ).astype(jnp.bfloat16)
    hidden_two = jax.nn.silu(
        jnp.dot(hidden_one, w_second, preferred_element_type=jnp.float32)
    ).astype(jnp.bfloat16)
    return jnp.dot(hidden_two, w_third, preferred_element_type=jnp.float32)


def flip_pieces(received):
    dims = received.shape
    return jnp.swapaxes(received, 3, 4).reshape(dims[0], dims[1], dims[2] * dims[4], dims[3])


def right_rows(band_rows):
    return with_halo(band_rows, (("rows", 0),), BAND // 2)


def band_product(left_band, right_band):
    half_band = BAND // 2
    tile_rows = left_band.shape[0]
    initial = jnp.zeros(left_band.shape, jnp.float32)
    summed = initial
    column_piece = lax.all_gather(left_band, "feat", axis=3, tiled=True)
    for offset in range(BAND):
        lower_slot = max(0, offset - half_band)
        upper_slot = min(BAND, offset + half_band + 1)
        product = jnp.einsum(
            "irm,icmk->icrk",
            column_piece[:, offset],
            right_band[
                offset : offset + tile_rows,
                lower_slot - offset + half_band : upper_slot - offset + half_band,
            ],
            precision=lax.Precision.HIGHEST,
            preferred_element_type=jnp.float32,
        )
        summed = summed.at[:, lower_slot:upper_slot].add(product)
    return summed


def local(edge_feats, edge_owner, src_local, band_slot, dst_local, w_first, w_second, w_third):
    feat_count = lax.axis_size("feat")
    row_count = lax.axis_size("rows")
    group_index = lax.axis_index("feat")
    edge_count = edge_feats.shape[0]
    capacity = max(2, 2 * edge_count // row_count)
    blocks_tile = TILE // BLOCK
    group_cols = BLOCK // feat_count
    col_width = TILE // feat_count
    half_band = BAND // 2
    values = edge_values(edge_feats, w_first, w_second, w_third)
    pieces = values.reshape(edge_count, feat_count, BLOCK * group_cols)
    owner_row = edge_owner[:, 0]
    onehot = (owner_row[:, None] == jnp.arange(row_count, dtype=jnp.int32)[None, :]).astype(
        jnp.int32
    )
    slot_index = jnp.sum(jnp.cumsum(onehot, axis=0) * onehot, axis=1) - 1
    target = owner_row * capacity + slot_index
    record_code = src_local * (BAND * blocks_tile) + band_slot * blocks_tile + dst_local
    send_vals = (
        jnp.zeros((row_count * capacity, feat_count, BLOCK * group_cols), jnp.float32)
        .at[target]
        .set(pieces)
    )
    send_codes = jnp.full((row_count * capacity,), -1, jnp.int32).at[target].set(record_code)
    send_codes = jnp.broadcast_to(send_codes[:, None], (row_count * capacity, feat_count))
    send_vals = send_vals.reshape(row_count, capacity, feat_count, BLOCK * group_cols)
    send_codes = send_codes.reshape(row_count, capacity, feat_count)
    got_vals, got_codes = (
        lax.all_to_all(
            lax.all_to_all(send_vals, "rows", split_axis=0, concat_axis=0, tiled=True),
            "feat",
            split_axis=2,
            concat_axis=2,
            tiled=True,
        ),
        lax.all_to_all(
            lax.all_to_all(send_codes, "rows", split_axis=0, concat_axis=0, tiled=True),
            "feat",
            split_axis=2,
            concat_axis=2,
            tiled=True,
        ),
    )
    record_codes = got_codes.reshape(-1)
    record_vals = got_vals.reshape(record_codes.shape[0], BLOCK * group_cols)
    entries = jnp.arange(BLOCK * group_cols, dtype=jnp.int32)
    component = entries // group_cols
    unit_col = entries % group_cols
    source = record_codes // (BAND * blocks_tile)
    slot_band = record_codes // blocks_tile % BAND
    dest_block = record_codes % blocks_tile
    tile_row = source // blocks_tile
    src_block = source % blocks_tile
    row_pos = (
        (component // group_cols)[None, :] * col_width
        + src_block[:, None] * group_cols
        + (component % group_cols)[None, :]
    )
    col_pos = dest_block[:, None] * group_cols + unit_col[None, :]
    flat_index = ((tile_row * BAND + slot_band)[:, None] * TILE + row_pos) * col_width + col_pos
    total_size = TILE_DEV * BAND * TILE * col_width
    flat_index = jnp.where(record_codes[:, None] >= 0, flat_index, total_size)
    hamil = (
        jnp.zeros((total_size,), jnp.float32)
        .at[flat_index.reshape(-1)]
        .add(record_vals.reshape(-1), mode="drop")
    )
    hamil = hamil.reshape(TILE_DEV, BAND, TILE, col_width)
    degree = feat_count * edge_count / (TILE_DEV * blocks_tile)
    sym_scale = 0.5 * (0.5 / math.sqrt(2.0 * BLOCK * degree))
    identity_cols = (
        jnp.arange(TILE, dtype=jnp.int32)[:, None]
        == group_index * col_width + jnp.arange(col_width, dtype=jnp.int32)[None, :]
    ).astype(jnp.float32)
    widened = with_halo(hamil, (("rows", 0),), half_band)
    partner = jnp.stack(
        [
            widened[slot_index : slot_index + TILE_DEV, BAND - 1 - slot_index]
            for slot_index in range(BAND)
        ],
        axis=1,
    )
    split_rows = partner.reshape(TILE_DEV, BAND, feat_count, col_width, col_width)
    received = lax.all_to_all(split_rows, "feat", split_axis=2, concat_axis=2, tiled=True)
    start = sym_scale * (hamil + flip_pieces(received))
    start = start.at[:, half_band].add(0.5 * identity_cols)
    start_right = right_rows(start)
    squared = band_product(start, start_right)
    purified = 2.0 * squared - band_product(squared, right_rows(squared))
    return jnp.swapaxes(purified, 2, 3)


def solution(mesh):
    in_specs = (
        P(("rows", "feat"), None),
        P(("rows", "feat"), None),
        P(("rows", "feat")),
        P(("rows", "feat")),
        P(("rows", "feat")),
        P(),
        P(),
        P(),
    )
    out_specs = P("rows", None, "feat", None)
    return jax.shard_map(local, mesh=mesh, in_specs=in_specs, out_specs=out_specs, check_vma=False)
```

profile of v0, /device:TPU:9, one launch (start us, length us, event | category | flops | bytes accessed | tf_op | source)
XLA Modules:
  0.0 1180.6 jit_solution(3920735610285878600)
XLA Ops:
  12.4 5.7 all-to-all-start
  24.3 5.3 all-to-all-start.1
  30.0 7.0 scatter_fusion
  38.6 4.6 all-to-all-start.2
  46.2 9.0 all-to-all-done.2
  59.7 5.9 all-to-all-start.3
  66.1 7.4 all-to-all-done.3
  73.5 2.1 reduce.43
  77.4 749.4 %scatter_custom_fusion.2 = f32[294912]{0:T(1024)S(1)} fusion(s32[131072]{0:T(1024)S(1)} %bitcast.271, f32[131072]{0:T(1024)S(1)} %reshape.996, f32[]{:T(128)} %constant.571.clone.1), kind=kCustom, calls=%fused_computation.52 | custom fusion | flops 131072 | bytes 1179652 | tf_op jit(solution)/shard_map/scatter-add | solution.py:136
  826.9 2.0 slice.741
  828.8 3.1 copy.125
  832.0 2.0 slice.748
  833.9 3.1 copy.127
  837.0 2.4 collective-permute-start.1
  839.4 2.7 reshape.970
  842.1 3.0 copy.126
  850.4 10.6 collective-permute-done.1
  863.6 4.8 reshape.971
  868.4 5.3 copy.206
  873.7 5.1 reshape.1031
  878.8 4.0 all-to-all-start.4
  883.0 14.7 %all-to-all-done.4 = f32[4,1,73728]{2,1,0:T(1,128)S(1)} async-done(((f32[4,1,73728]{2,1,0:T(1,128)}), f32[4,1,73728]{2,1,0:T(1,128)S(1)}, u32[]{:S(2)}, u32[]{:S(2)}) %all-to-all-start.4) | async-done | bytes 1179680 | tf_op jit(solution)/shard_map/all_to_all | solution.py:154
  897.7 4.0 reduce.44
  901.8 3.8 reshape.1032
  905.6 3.3 bitcast_bitcast_fusion
  910.0 3.2 fusion
  915.1 4.8 copy.134
  920.0 4.2 fusion.72
  924.3 3.2 copy.132
  927.4 6.6 collective-permute-start.2
  934.0 3.8 copy.133
  939.4 70.4 %collective-permute-start.3 = (f32[4,9,128,32]{2,3,1,0:T(8,128)}, f32[4,9,128,32]{2,3,1,0:T(8,128)}, u32[]{:S(2)}, u32[]{:S(2)}) collective-permute-start(f32[4,9,128,32]{2,3,1,0:T(8,128)} %copy.141), channel_id=1, source_target_pairs={{4,0},{8,4},{12,8},{16,12},{20,16},{24,20},{28,24},{0,28},{5,1},{9... | collective-permute-start | bytes 1769480 | tf_op jit(solution)/shard_map/ppermute | solution.py:23
  1009.8 68.9 %all-gather.3.cloned.1.call-done = f32[8,9,128,128]{2,0,1,3:T(8,128)} async-done(((f32[8,9,128,32]{2,0,1,3:T(8,128)}), f32[8,9,128,128]{2,0,1,3:T(8,128)}) %all-gather.3.cloned.1.call-update) | async-done | bytes 4718608 | tf_op jit(solution)/shard_map/all_gather | solution.py:52
  1078.7 3.9 fusion.71
  1082.8 2.3 convolution_bitcast_fusion.17
  1085.2 2.1 copy.194
  1087.3 2.1 copy.195
  1089.3 2.1 copy.196
  1093.5 2.6 add_dynamic-update-slice_fusion.1
  1096.1 2.2 fusion.12
  1098.3 2.2 fusion.4
  1100.5 9.5 fusion.2
  1110.1 2.0 fusion.5
  1116.0 2.5 constant_dynamic-update-slice_fusion.5
  1118.5 2.1 constant_dynamic-update-slice_fusion.4
  1120.6 2.2 fusion.14
  1127.9 23.7 %collective-permute-done.4 = f32[4,9,128,32]{2,3,1,0:T(8,128)S(1)} collective-permute-done((f32[4,9,128,32]{2,3,1,0:T(8,128)S(1)}, f32[4,9,128,32]{2,3,1,0:T(8,128)S(1)}, u32[]{:S(2)}, u32[]{:S(2)}) %collective-permute-start.4) | collective-permute-done | bytes 589856 | tf_op jit(solution)/shard_map/ppermute | solution.py:20
  1151.6 9.8 all-gather.5.cloned.1.call-done
  (128 shorter events, 60.0 us)
Async XLA Ops:
  6.5 11.6 copy-start
  12.4 9.8 all-to-all-start
  24.3 14.3 %all-to-all-start.1 = ((s32[4,1,512]{2,1,0:T(1,128)}), s32[4,1,512]{2,1,0:T(1,128)S(1)}, u32[]{:S(2)}, u32[]{:S(2)}) async-start(s32[4,1,512]{2,1,0:T(1,128)} %reshape.1025), calls=%async_computation.1 | async-start | bytes 16384 | tf_op jit(solution)/shard_map/all_to_all | solution.py:106
  38.6 16.6 %all-to-all-start.2 = ((f32[8,1,16384]{2,1,0:T(1,128)}), f32[8,1,16384]{2,1,0:T(1,128)S(1)}, u32[]{:S(2)}, u32[]{:S(2)}) async-start(f32[8,1,16384]{2,1,0:T(1,128)} %reshape.1027), calls=%async_computation.2 | async-start | bytes 1048576 | tf_op jit(solution)/shard_map/all_to_all | solution.py:100
  59.7 13.8 %all-to-all-start.3 = ((f32[4,1,32768]{2,1,0:T(1,128)}), f32[4,1,32768]{2,1,0:T(1,128)S(1)}, u32[]{:S(2)}, u32[]{:S(2)}) async-start(f32[4,1,32768]{2,1,0:T(1,128)} %reshape.1029), calls=%async_computation.3 | async-start | bytes 1048576 | tf_op jit(solution)/shard_map/all_to_all | solution.py:99
  832.0 15.1 %collective-permute-start = (f32[4,9,128,32]{2,3,1,0:T(8,128)}, f32[4,9,128,32]{2,3,1,0:T(8,128)S(1)}, u32[]{:S(2)}, u32[]{:S(2)}) collective-permute-start(f32[4,9,128,32]{2,3,1,0:T(8,128)} %copy.125), channel_id=1, source_target_pairs={{0,4},{4,8},{8,12},{12,16},{16,20},{20,24},{24,28},{28,0},{1,5},{5... | collective-permute-start | bytes 1769480 | tf_op jit(solution)/shard_map/ppermute | solution.py:20
  837.0 23.9 %collective-permute-start.1 = (f32[4,9,128,32]{2,3,1,0:T(8,128)}, f32[4,9,128,32]{2,3,1,0:T(8,128)S(1)}, u32[]{:S(2)}, u32[]{:S(2)}) collective-permute-start(f32[4,9,128,32]{2,3,1,0:T(8,128)} %copy.127), channel_id=1, source_target_pairs={{4,0},{8,4},{12,8},{16,12},{20,16},{24,20},{28,24},{0,28},{5,1},{9... | collective-permute-start | bytes 1769480 | tf_op jit(solution)/shard_map/ppermute | solution.py:23
  845.1 1.0 slice-start.2
  878.8 19.0 %all-to-all-start.4 = ((f32[4,1,73728]{2,1,0:T(1,128)}), f32[4,1,73728]{2,1,0:T(1,128)S(1)}, u32[]{:S(2)}, u32[]{:S(2)}) async-start(f32[4,1,73728]{2,1,0:T(1,128)} %reshape.1031), calls=%async_computation.4 | async-start | bytes 2359296 | tf_op jit(solution)/shard_map/all_to_all | solution.py:154
  882.7 195.9 %all-gather.3.cloned.1.call-start = ((), (), s32[]{:S(2)}) async-start(), calls=%async_computation.5 | async-start | bytes 5898240 | tf_op jit(solution)/shard_map/all_gather | solution.py:52
  905.6 3.9 slice-start
  908.9 1.1 slice-start.1
  920.0 241.4 %all-gather.5.cloned.1.call-start = ((), (), s32[]{:S(2)}) async-start(), calls=%async_computation.6 | async-start | bytes 5898240 | tf_op jit(solution)/shard_map/all_gather | solution.py:52
  927.4 155.4 %collective-permute-start.2 = (f32[4,9,128,32]{2,3,1,0:T(8,128)}, f32[4,9,128,32]{2,3,1,0:T(8,128)}, u32[]{:S(2)}, u32[]{:S(2)}) collective-permute-start(f32[4,9,128,32]{2,3,1,0:T(8,128)} %copy.132), channel_id=1, source_target_pairs={{0,4},{4,8},{8,12},{12,16},{16,20},{20,24},{24,28},{28,0},{1,5},{5... | collective-permute-start | bytes 1769480 | tf_op jit(solution)/shard_map/ppermute | solution.py:20
  939.4 170.7 %collective-permute-start.3 = (f32[4,9,128,32]{2,3,1,0:T(8,128)}, f32[4,9,128,32]{2,3,1,0:T(8,128)}, u32[]{:S(2)}, u32[]{:S(2)}) collective-permute-start(f32[4,9,128,32]{2,3,1,0:T(8,128)} %copy.141), channel_id=1, source_target_pairs={{4,0},{8,4},{12,8},{16,12},{20,16},{24,20},{28,24},{0,28},{5,1},{9... | collective-permute-start | bytes 1769480 | tf_op jit(solution)/shard_map/ppermute | solution.py:23
  1093.5 2.6 copy-start.6
  1093.5 2.6 copy-start.12
  1096.1 2.2 copy-start.11
  1098.3 2.2 copy-start.5
  1100.5 9.5 copy-start.9
  1112.0 1.0 copy-start.8
  1112.0 1.4 copy-start.4
  1114.5 1.5 copy-start.7
  1116.0 2.5 copy-start.10
  1122.8 1.0 copy-start.2
  1123.8 37.6 %copy-start.3 = (f32[8,9,128,32]{2,3,1,0:T(8,128)S(1)}, f32[8,9,128,32]{2,3,1,0:T(8,128)}, u32[]{:S(2)}) copy-start(f32[8,9,128,32]{2,3,1,0:T(8,128)} %copy-done.2) | copy-start | bytes 3538948
  1125.3 26.4 %collective-permute-start.4 = (f32[4,9,128,32]{2,3,1,0:T(8,128)S(1)}, f32[4,9,128,32]{2,3,1,0:T(8,128)S(1)}, u32[]{:S(2)}, u32[]{:S(2)}) collective-permute-start(f32[4,9,128,32]{2,3,1,0:T(8,128)S(1)} %get-tuple-element.261), channel_id=1, source_target_pairs={{0,4},{4,8},{8,12},{12,16},{16,20},{20,24},{24,28},{28,0},{1,5},{5... | collective-permute-start | bytes 1769480 | tf_op jit(solution)/shard_map/ppermute | solution.py:20
  1126.5 41.9 %collective-permute-start.5 = (f32[4,9,128,32]{2,3,1,0:T(8,128)S(1)}, f32[4,9,128,32]{2,3,1,0:T(8,128)S(1)}, u32[]{:S(2)}, u32[]{:S(2)}) collective-permute-start(f32[4,9,128,32]{2,3,1,0:T(8,128)S(1)} %get-tuple-element.260), channel_id=1, source_target_pairs={{4,0},{8,4},{12,8},{16,12},{20,16},{24,20},{28,24},{0,28},{5,1},{9... | collective-permute-start | bytes 1769480 | tf_op jit(solution)/shard_map/ppermute | solution.py:23
  1161.4 2.5 copy-start.13
  1171.5 2.1 copy-start.1
Sparse Core Ops, SparseCore 0:
  920.1 158.5 all-gather.2
  1124.0 37.4 all-gather.4
where the time goes:
time: 1190 us; the launch traced here: 1180 us
  other arithmetic  776 us (65%)
  waiting for transfers between devices  147 us (12%)
  starting transfers between devices  108 us (9%)
  local copies, waits for them, and re-layouts  96.2 us (8%)
  matrix products  40 us (3%)
  between operations  14.2 us (1%)
    scatter-add x1, other arithmetic, local(): hamil = jnp.zeros((total_size,), jnp.float32).at[flat_index.reshape(-1)]....  749 us
    all_gather x2, waiting for transfers between devices, band_product(): column_piece = lax.all_gather(left_band, 'feat', axis=3, tiled=True)  78.7 us
    ppermute x3, starting transfers between devices, with_halo(): lax.ppermute(lax.slice_in_dim(block, 0, width, axis=dim), axis, backward)  74.2 us
    dot_general x18, matrix products, band_product(): jnp.einsum('irm,icmk->icrk', column_piece[:, offset], right_band[offset:o...  37.6 us
    unnamed x54, local copies, waits for them, and re-layouts  29.3 us
    ppermute x3, waiting for transfers between devices, with_halo(): lax.ppermute(lax.slice_in_dim(block, block.shape[dim] - width, None, axis...  24.5 us
  transfers between devices with their start and end apart: 13, of which 9 were waited for; matrix products, arithmetic and copies ran while one was open for 7% of the time, Pallas kernels for 0%

commit v1 on v0

v1 whole, which is shorter than its diff:
```python
import functools
import math

import jax
import jax.numpy as jnp
import numpy as np
from jax import lax
from jax.experimental import pallas as pl
from jax.experimental.pallas import tpu as pltpu
from jax.sharding import PartitionSpec as P

BLOCK = 16
TILE = 128
BAND = 9
TILE_DEV = 8
HALF = BAND // 2
NB = TILE // BLOCK
WIN = TILE_DEV + 2 * HALF
NT = TILE_DEV * BAND
LANES = 128
CODE_LANE = 112
MESH = pl.DeviceIdType.MESH
f32 = jnp.float32
bf16 = jnp.bfloat16


def split2(x):
    hi = x.astype(bf16)
    return hi, (x - hi.astype(f32)).astype(bf16)


def mm(a, b):
    return jnp.dot(a, b, preferred_element_type=f32)


def piece_columns(groups, cols):
    per = BLOCK * cols
    sub = cols * cols
    perm = np.zeros((BLOCK * BLOCK, groups * LANES), np.float32)
    for g in range(groups):
        for k in range(per):
            perm[g * per + k, g * LANES + k] = 1
        at = g * LANES + per
        for other in range(groups):
            if other != g:
                for k in range(sub):
                    perm[other * per + g * sub + k, at + k] = 1
                at += sub
    return perm


def spread_columns(groups, cols):
    per = BLOCK * cols
    sub = cols * cols
    width = TILE // groups
    by_col = np.zeros((LANES, cols * TILE), np.float32)
    by_row = np.zeros((groups, LANES, cols * TILE), np.float32)
    for u in range(cols):
        for lane in range(TILE):
            comp = lane // width * cols + lane % cols
            by_col[comp * cols + u, u * TILE + lane] = 1
            for g in range(groups):
                other = lane // width
                if other == g:
                    k = (g * cols + u) * cols + lane % cols
                else:
                    k = per + (other - (other > g)) * sub + u * cols + lane % cols
                by_row[g, k, u * TILE + lane] = 1
    return by_col, by_row


def route_kernel(rows, cap, groups, feats, owner_row, code_col, w1, w2, w3, perm, out):
    edges = feats.shape[0]
    h1 = mm(feats[...], w1[...])
    h1 = (h1 / (1.0 + jnp.exp(-h1))).astype(bf16)
    h2 = mm(h1, w2[...])
    h2 = (h2 / (1.0 + jnp.exp(-h2))).astype(bf16)
    w3p = mm(w3[...], perm[...]).astype(bf16)
    vals = mm(h2, w3p)
    lane = lax.broadcasted_iota(jnp.int32, vals.shape, 1)
    vals = jnp.where(lane % LANES == CODE_LANE, code_col[...].astype(f32), vals)
    owner = owner_row[...]
    names = (owner == lax.broadcasted_iota(jnp.int32, (rows, edges), 0)).astype(f32)
    before = (
        lax.broadcasted_iota(jnp.int32, (edges, edges), 0)
        < lax.broadcasted_iota(jnp.int32, (edges, edges), 1)
    ).astype(bf16)
    rank = jnp.sum(names * mm(names.astype(bf16), before), axis=0, keepdims=True).astype(jnp.int32)
    target = owner * cap + rank
    place = (target == lax.broadcasted_iota(jnp.int32, (rows * cap, edges), 0)).astype(bf16)
    hi, lo = split2(vals)
    sent = mm(place, hi) + mm(place, lo)
    for g in range(groups):
        part = sent[:, g * LANES : (g + 1) * LANES]
        out[:, g] = part.reshape(rows, cap, LANES)


def own_tiles():
    return [(i, j) for i in range(TILE_DEV) for j in range(TILE_DEV) if abs(i - j) <= HALF]


def tile_at(i, j):
    return i * BAND + j - i + HALF


LOW = [(a, b) for a in range(HALF) for b in range(HALF)]
LOW_PART = [(j, i) for j in range(HALF) for i in range(j - HALF, 0)]
HIGH_PART = [
    (j, i) for j in range(TILE_DEV - HALF, TILE_DEV) for i in range(TILE_DEV, j + HALF + 1)
]
CORNER = len(LOW)
E_HALO = CORNER + len(LOW_PART)


def band_kernel(
    rows, groups, scale,
    rec, by_col, by_row, out,
    dh, rh, ge, gw, se, re, sw, rw, bhi, blo, ahi, alo, t0, t1, s_sem, r_sem,
):
    r = lax.axis_index("rows")
    g = lax.axis_index("feat")
    width = TILE // groups
    cols = BLOCK // groups
    up, down = lax.rem(r + 1, rows), lax.rem(r + rows - 1, rows)
    y, c = g // 2, g % 2
    by_slot = [g, y * 2 + (1 - c), (1 - y) * 2 + c, (1 - y) * 2 + (1 - c)]
    core_peer, y_peer = by_slot[1], by_slot[2]

    barrier = pltpu.get_barrier_semaphore()
    for who in ((up, g), (down, g), (r, core_peer), (r, y_peer)):
        pl.semaphore_signal(barrier, inc=1, device_id=who, device_id_type=MESH)
    pl.semaphore_wait(barrier, 4)

    x = rec[...]
    count = x.shape[0]
    code_c = x[:, CODE_LANE : CODE_LANE + 1].astype(jnp.int32)
    code_r = x.T[CODE_LANE : CODE_LANE + 1, :].astype(jnp.int32)
    hi, lo = split2(x)
    lane = lax.broadcasted_iota(jnp.int32, (count, cols * TILE), 1)
    lane_block = lane % width // cols
    tile_id = lax.shift_right_logical(code_r, 10) % 8 * BAND + lax.shift_right_logical(code_r, 3) % 16
    valid = code_r >= 8192
    src_r, dst_r = lax.shift_right_logical(code_r, 7) % 8, code_r % 8
    src_c, dst_c = lax.shift_right_logical(code_c, 7) % 8, code_c % 8
    line = lax.broadcasted_iota(jnp.int32, (NT * NB, count), 0)
    for dest, spread, row_block, lane_of in (
        (dh, by_col, dst_r, src_c),
        (rh, by_row, src_r, dst_c),
    ):
        index = jnp.where(valid, tile_id * NB + row_block, -1)
        place = (line == index).astype(bf16)
        keep = lane_block == lane_of
        strips_hi = jnp.where(keep, mm(hi, spread[...]), 0.0).astype(bf16)
        strips_lo = jnp.where(keep, mm(lo, spread[...]), 0.0).astype(bf16)
        total = mm(place, strips_hi) + mm(place, strips_lo)
        for u in range(cols):
            dest[:, pl.ds(u, NB, stride=cols), :] = total[:, u * TILE : (u + 1) * TILE].reshape(
                NT, NB, TILE
            )

    zero_block = jnp.zeros((TILE, TILE), bf16)
    for p in range(TILE_DEV // 2):
        for i, kk in ((2 * p, 2 * p + 9), (2 * p + 1, 2 * p)):
            for ref in (bhi, blo):
                ref[kk * TILE : (kk + 1) * TILE, i * TILE : (i + 1) * TILE] = zero_block
    ahi[...] = jnp.zeros(ahi.shape, bf16)
    alo[...] = jnp.zeros(alo.shape, bf16)

    def copy(src, dst, sem, who):
        return pltpu.make_async_remote_copy(
            src_ref=src, dst_ref=dst, send_sem=s_sem.at[sem], recv_sem=r_sem.at[sem],
            device_id=who, device_id_type=MESH,
        )

    def gather(buf, base):
        near = copy(buf.at[0], buf.at[1], base, (r, core_peer))
        far = copy(buf.at[0], buf.at[2], base + 1, (r, y_peer))
        near.start()
        far.start()
        far.wait_recv()
        on = copy(buf.at[2], buf.at[3], base + 2, (r, core_peer))
        on.start()
        near.wait_recv()
        on.wait_recv()
        return [near, far, on]

    def pack_corners(send, buf):
        for n, (a, b) in enumerate(LOW):
            send[0, n] = buf[0, tile_at(a, b)]
            send[1, n] = buf[0, tile_at(a + HALF, b + HALF)]

    def exchange(send, recv, base):
        to_low = copy(send.at[0], recv.at[1], base, (down, g))
        to_high = copy(send.at[1], recv.at[0], base + 1, (up, g))
        to_low.start()
        to_high.start()
        return [to_low, to_high]

    def put_a(jj, kk, val):
        h, l = split2(val)
        ahi[jj * width : (jj + 1) * width, kk * TILE : (kk + 1) * TILE] = h
        alo[jj * width : (jj + 1) * width, kk * TILE : (kk + 1) * TILE] = l

    halo_tiles = [
        (j, kk) for j in range(TILE_DEV) for kk in list(range(HALF)) + list(range(WIN - HALF, WIN))
        if 0 <= kk - j < BAND
    ]

    def build(buf, halos):
        for i in range(TILE_DEV):
            for s in range(BAND):
                for slot in range(4):
                    h, l = split2(buf[slot, i * BAND + s])
                    at = pl.multiple_of((i + s) * TILE + by_slot[slot] * width, width)
                    bhi[pl.ds(at, width), i * TILE : (i + 1) * TILE] = h
                    blo[pl.ds(at, width), i * TILE : (i + 1) * TILE] = l
                put_a(i + s, i + HALF, buf[0, i * BAND + s])
        for n, (a, b) in enumerate(LOW):
            put_a(b, a, halos[0, n])
            put_a(b + WIN - HALF, a + WIN - HALF, halos[1, n])
        for n, (j, kk) in enumerate(halo_tiles):
            for slot in range(4):
                at = pl.multiple_of(by_slot[slot] * width, width)
                t0[n, pl.ds(at, width), :] = buf[slot, j * BAND + kk - j]
        for n, (j, kk) in enumerate(halo_tiles):
            t1[n] = t0[n].T
        for n, (j, kk) in enumerate(halo_tiles):
            put_a(j + HALF, kk, t1[n, pl.ds(pl.multiple_of(g * width, width), width), :])

    def product(emit):
        for p in range(TILE_DEV // 2):
            rows_at = slice(2 * p * width, (2 * p + 10) * width)
            mid = slice(2 * p * TILE, (2 * p + 10) * TILE)
            cols_at = slice(2 * p * TILE, (2 * p + 2) * TILE)
            a_h, b_h = ahi[rows_at, mid], bhi[mid, cols_at]
            acc = mm(a_h, b_h) + mm(a_h, blo[mid, cols_at]) + mm(alo[rows_at, mid], b_h)
            for di in range(2):
                for s in range(BAND):
                    m = s + di
                    emit(2 * p + di, s, acc[m * width : (m + 1) * width, di * TILE : (di + 1) * TILE])

    for i, j in own_tiles():
        ge[0, tile_at(i, j)] = scale * (dh[tile_at(i, j)] + rh[tile_at(j, i)])
    pack_corners(se, ge)
    for n, (j, i) in enumerate(LOW_PART):
        se[0, CORNER + n] = rh[tile_at(j, i)]
    for n, (j, i) in enumerate(HIGH_PART):
        se[1, CORNER + n] = rh[tile_at(j, i)]
    pending = exchange(se, re, 0)
    for item in pending:
        item.wait_recv()
    for n, (j, i) in enumerate(HIGH_PART):
        own, halo = i - TILE_DEV, j - TILE_DEV
        ge[0, tile_at(own, halo)] = scale * (dh[tile_at(own, halo)] + re[0, CORNER + n])
    for n, (j, i) in enumerate(LOW_PART):
        own, halo = i + TILE_DEV, j + TILE_DEV
        ge[0, tile_at(own, halo)] = scale * (dh[tile_at(own, halo)] + re[1, CORNER + n])
    pending += gather(ge, 2)
    build(ge, re)

    def first(i, s, acc):
        gw[0, i * BAND + s] = ge[0, i * BAND + s] + acc

    product(first)
    pack_corners(sw, gw)
    more = exchange(sw, rw, 5)
    pending += more
    pending += gather(gw, 7)
    for item in more:
        item.wait_recv()
    build(gw, rw)
    eye = (
        lax.broadcasted_iota(jnp.int32, (width, TILE), 0) + g * width
        == lax.broadcasted_iota(jnp.int32, (width, TILE), 1)
    ).astype(f32)

    def second(i, s, acc):
        val = 1.5 * gw[0, i * BAND + s] - acc
        if s == HALF:
            val = val + 0.4375 * eye
        out[i, s] = val

    product(second)
    for item in pending:
        item.wait_send()


def local(edge_feats, edge_owner, src_local, band_slot, dst_local, w_first, w_second, w_third):
    groups = lax.axis_size("feat")
    rows = lax.axis_size("rows")
    edges = edge_feats.shape[0]
    cap = max(2, 2 * edges // rows)
    cols = BLOCK // groups
    width = TILE // groups
    code = 8192 + src_local * 128 + band_slot * 8 + dst_local
    vm = pl.BlockSpec(memory_space=pltpu.VMEM)
    perm = jnp.asarray(piece_columns(groups, cols), bf16)
    by_col, by_row = spread_columns(groups, cols)
    by_col = jnp.asarray(by_col, bf16)
    by_row = jnp.asarray(by_row, bf16)[lax.axis_index("feat")]
    sent = pl.pallas_call(
        functools.partial(route_kernel, rows, cap, groups),
        out_shape=jax.ShapeDtypeStruct((rows, groups, cap, LANES), f32),
        in_specs=[vm] * 7,
        out_specs=vm,
        compiler_params=pltpu.CompilerParams(vmem_limit_bytes=32 << 20),
    )(edge_feats, edge_owner.reshape(1, edges), code.reshape(edges, 1), w_first, w_second, w_third, perm)
    sent = sent.reshape(rows * groups, cap, LANES)
    got = lax.all_to_all(sent, ("rows", "feat"), 0, 0, tiled=True)
    rec = got.reshape(rows * groups * cap, LANES)
    degree = groups * edges / (TILE_DEV * NB)
    scale = 0.5 * (0.5 / math.sqrt(2.0 * BLOCK * degree))
    tiles = (NT, width, TILE)
    return pl.pallas_call(
        functools.partial(band_kernel, rows, groups, scale),
        out_shape=jax.ShapeDtypeStruct((TILE_DEV, BAND, width, TILE), f32),
        in_specs=[vm] * 3,
        out_specs=vm,
        scratch_shapes=[
            pltpu.VMEM(tiles, f32),
            pltpu.VMEM(tiles, f32),
            pltpu.VMEM((4,) + tiles, f32),
            pltpu.VMEM((4,) + tiles, f32),
            pltpu.VMEM((2, E_HALO, width, TILE), f32),
            pltpu.VMEM((2, E_HALO, width, TILE), f32),
            pltpu.VMEM((2, CORNER, width, TILE), f32),
            pltpu.VMEM((2, CORNER, width, TILE), f32),
            pltpu.VMEM((WIN * TILE, TILE_DEV * TILE), bf16),
            pltpu.VMEM((WIN * TILE, TILE_DEV * TILE), bf16),
            pltpu.VMEM((WIN * width, WIN * TILE), bf16),
            pltpu.VMEM((WIN * width, WIN * TILE), bf16),
            pltpu.VMEM((20, TILE, TILE), f32),
            pltpu.VMEM((20, TILE, TILE), f32),
            pltpu.SemaphoreType.DMA((10,)),
            pltpu.SemaphoreType.DMA((10,)),
        ],
        compiler_params=pltpu.CompilerParams(
            collective_id=0, has_side_effects=True, vmem_limit_bytes=60 << 20
        ),
    )(rec, by_col, by_row)


def solution(mesh):
    in_specs = (
        P(("rows", "feat"), None),
        P(("rows", "feat"), None),
        P(("rows", "feat")),
        P(("rows", "feat")),
        P(("rows", "feat")),
        P(),
        P(),
        P(),
    )
    out_specs = P("rows", None, "feat", None)
    return jax.shard_map(local, mesh=mesh, in_specs=in_specs, out_specs=out_specs, check_vma=False)
```

time: 1190 us -> 144 us (0.12)
  other arithmetic: 776 us -> 0.72 us
  waiting for transfers between devices: 147 us -> 23.7 us
  Pallas kernels: 0 us -> 102 us
  starting transfers between devices: 108 us -> 6.36 us
  local copies, waits for them, and re-layouts: 96.2 us -> 10.3 us
  matrix products: 40 us -> 0 us
  between operations: 14.2 us -> 0.05 us
    scatter-add x2 -> x0, other arithmetic: 751 us -> none  [the longest x1 749 us: local(): hamil = jnp.zeros((total_size,), jnp.float32).at[flat_index.reshape(-1)]....]
    pallas_call x0 -> x2, Pallas kernels: none -> 102 us  [the longest x1 99.8 us: local(): pl.pallas_call(functools.partial(band_kernel, rows, groups, scale), out_s...]
    ppermute x6 -> x0, starting transfers between devices: 82 us -> none  [the longest x3 74.2 us: with_halo(): lax.ppermute(lax.slice_in_dim(block, 0, width, axis=dim), axis, backward)]
    all_gather x2 -> x0, waiting for transfers between devices: 78.7 us -> none  [band_product(): column_piece = lax.all_gather(left_band, 'feat', axis=3, tiled=True)]
    dot_general x20 -> x0, matrix products: 40 us -> none  [the longest x18 37.6 us: band_product(): jnp.einsum('irm,icmk->icrk', column_piece[:, offset], right_band[offset:o...]
    ppermute x6 -> x0, waiting for transfers between devices: 35.1 us -> none  [the longest x3 24.5 us: with_halo(): lax.ppermute(lax.slice_in_dim(block, block.shape[dim] - width, None, axis...]
    slice x13 -> x0, local copies, waits for them, and re-layouts: 25.6 us -> none  [the longest x6 12.3 us: with_halo(): lax.slice_in_dim(block, 0, width, axis=dim)]
    unnamed x54 -> x15, local copies, waits for them, and re-layouts: 29.3 us -> 8.58 us
  transfers between devices with their start and end apart: 13 -> 1, of which waited for: 9 -> 1; matrix products, arithmetic and copies ran while one was open for 7% -> 1% of each run, Pallas kernels for 0% -> 0%
where the time goes in v1:
time: 144 us; the launch traced here: 143 us
  Pallas kernels  102 us (71%)
  waiting for transfers between devices  23.7 us (16%)
  local copies, waits for them, and re-layouts  10.3 us (7%)
  starting transfers between devices  6.36 us (4%)
    pallas_call x1, Pallas kernels, local(): pl.pallas_call(functools.partial(band_kernel, rows, groups, scale), out_s...  99.8 us
    all_to_all x1, waiting for transfers between devices, local(): got = lax.all_to_all(sent, ('rows', 'feat'), 0, 0, tiled=True)  23.7 us
    unnamed x15, local copies, waits for them, and re-layouts  8.58 us
    all_to_all x1, starting transfers between devices, local(): got = lax.all_to_all(sent, ('rows', 'feat'), 0, 0, tiled=True)  6.36 us
  transfers between devices with their start and end apart: 1, of which 1 were waited for; matrix products, arithmetic and copies ran while one was open for 1% of the time, Pallas kernels for 0%

profile of v1, /device:TPU:9, one launch (start us, length us, event | category | flops | bytes accessed | tf_op | source)
XLA Modules:
  0.0 142.9 jit_solution(1011516653840342981)
XLA Ops:
  0.0 0.7 add_add_fusion
  0.7 0.1 copy.12.code_col
  0.9 0.0 copy-start
  0.9 0.9 copy-done
  1.8 0.0 copy-start.1
  1.8 0.9 copy-done.1
  2.7 0.0 copy-start.2
  2.7 0.9 copy-done.2
  3.6 0.0 copy-start.3
  3.6 0.9 copy-done.3
  4.5 0.0 copy-start.4
  4.5 0.9 copy-done.4
  5.4 0.0 copy-start.5
  5.4 0.7 copy-done.5
  6.1 2.0 %shard_map.109 = f32[8,4,64,128]{3,2,1,0:T(8,128)} custom-call(bf16[256,256]{1,0:T(8,128)(2,1)S(1)} %copy-done.1, s32[1,256]{1,0:T(1,128)S(1)} %bitcast.6, s32[256,1]{1,0:T(8,128)S(1)} %copy.12.code_col, bf16[256,256]{1,0:T(8,128)(2,1)S(1)} %copy-done.2, bf16[256,256]{1,0:T(8,128)(2,1)S(1)} %copy-done.3, bf16[256,256]{1,0:T(8,128)(2,1)S(1)} %copy-done.4, ...), custom_call_target="tpu_custom_call" | custom-call | tf_op jit(solution)/shard_map/pallas_call | solution.py:301
  8.1 6.4 %all-to-all-start = ((f32[32,64,128]{2,1,0:T(8,128)}), f32[32,64,128]{2,1,0:T(8,128)S(1)}, u32[]{:S(2)}, u32[]{:S(2)}) async-start(f32[32,64,128]{2,1,0:T(8,128)} %bitcast.2), calls=%async_computation | async-start | bytes 2097152 | tf_op jit(solution)/shard_map/all_to_all | solution.py:309
  14.4 1.6 %dynamic-slice_bitcast_fusion.by_row = bf16[128,512]{1,0:T(8,128)(2,1)} fusion(bf16[4,128,512]{2,1,0:T(8,128)(2,1)} %constant.22.clone, s32[]{:T(128)S(6)} %select_n.3), kind=kLoop, calls=%fused_computation | loop fusion | bytes 262148 | tf_op jit(solution)/shard_map/squeeze | solution.py:300
  16.0 23.7 %all-to-all-done = f32[32,64,128]{2,1,0:T(8,128)S(1)} async-done(((f32[32,64,128]{2,1,0:T(8,128)}), f32[32,64,128]{2,1,0:T(8,128)S(1)}, u32[]{:S(2)}, u32[]{:S(2)}) %all-to-all-start) | async-done | bytes 1048608 | tf_op jit(solution)/shard_map/all_to_all | solution.py:309
  39.7 0.0 copy-start.6
  39.7 1.0 copy-done.6
  40.7 99.8 %shard_map.110 = f32[8,9,32,128]{3,2,1,0:T(8,128)} custom-call(f32[2048,128]{1,0:T(8,128)} %bitcast.7, bf16[128,512]{1,0:T(8,128)(2,1)} %constant.21.clone.by_col, bf16[128,512]{1,0:T(8,128)(2,1)} %dynamic-slice_bitcast_fusion.by_row), custom_call_target="tpu_custom_call" | custom-call | tf_op jit(solution)/shard_map/pallas_call | solution.py:314
  140.5 2.4 %copy.14 = f32[8,9,32,128]{3,2,1,0:T(8,128)} copy(f32[8,9,32,128]{3,2,1,0:T(8,128)} %shard_map.110) | data formatting | bytes 2359296
Async XLA Ops:
  0.9 1.0 copy-start
  1.8 0.9 copy-start.1
  2.7 0.9 copy-start.2
  3.6 0.9 copy-start.3
  4.5 0.9 copy-start.4
  5.4 0.7 copy-start.5
  8.1 31.6 %all-to-all-start = ((f32[32,64,128]{2,1,0:T(8,128)}), f32[32,64,128]{2,1,0:T(8,128)S(1)}, u32[]{:S(2)}, u32[]{:S(2)}) async-start(f32[32,64,128]{2,1,0:T(8,128)} %bitcast.2), calls=%async_computation | async-start | bytes 2097152 | tf_op jit(solution)/shard_map/all_to_all | solution.py:309
  39.7 1.0 copy-start.6

commit v2 on v1

v2 whole, which is shorter than its diff:
```python
import functools
import math

import jax
import jax.numpy as jnp
from jax import lax
from jax.experimental import pallas as pl
from jax.experimental.pallas import tpu as pltpu
from jax.sharding import PartitionSpec as P

BLOCK = 16
TILE = 128
BAND = 9
TILE_DEV = 8
HALF = BAND // 2
NB = TILE // BLOCK
WIN = TILE_DEV + 2 * HALF
NT = TILE_DEV * BAND
LANES = 128
CODE_LANE = 112
MESH = pl.DeviceIdType.MESH
f32 = jnp.float32
bf16 = jnp.bfloat16


def split2(x):
    hi = x.astype(bf16)
    return hi, (x - hi.astype(f32)).astype(bf16)


def mm(a, b):
    return jnp.dot(a, b, preferred_element_type=f32)


def piece_columns(groups, cols):
    per = BLOCK * cols
    sub = cols * cols
    shape = (BLOCK * BLOCK, groups * LANES)
    source = lax.broadcasted_iota(jnp.int32, shape, 0)
    lane = lax.broadcasted_iota(jnp.int32, shape, 1)
    g, k = lane // LANES, lane % LANES
    other = (k - per) // sub
    other = other + (other >= g).astype(jnp.int32)
    from_row = other * per + g * sub + (k - per) % sub
    want = jnp.where(k < per, g * per + k, jnp.where(k < CODE_LANE, from_row, -1))
    return (source == want).astype(bf16)


def spread_columns(groups, cols, g):
    per = BLOCK * cols
    sub = cols * cols
    width = TILE // groups
    shape = (LANES, cols * TILE)
    source = lax.broadcasted_iota(jnp.int32, shape, 0)
    full = lax.broadcasted_iota(jnp.int32, shape, 1)
    u, lane = full // TILE, full % TILE
    other, unit = lane // width, lane % cols
    by_col = source == (other * cols + unit) * cols + u
    apart = per + (other - (other > g).astype(jnp.int32)) * sub + u * cols + unit
    by_row = source == jnp.where(other == g, (g * cols + u) * cols + unit, apart)
    return by_col.astype(bf16), by_row.astype(bf16)


def route_kernel(
    rows, cap, groups, feats_in, owner_in, code_in, w1_in, w2_in, w3_in, out,
    feats, owner_row, code_col, w1, w2, w3, sems,
):
    fetches = []
    for n, (src, dst) in enumerate(
        ((feats_in, feats), (w1_in, w1), (w2_in, w2), (w3_in, w3), (owner_in, owner_row), (code_in, code_col))
    ):
        fetch = pltpu.make_async_copy(src, dst, sems.at[n])
        fetch.start()
        fetches.append(fetch)
    edges = feats.shape[0]
    perm = piece_columns(groups, BLOCK // groups)
    before = (
        lax.broadcasted_iota(jnp.int32, (edges, edges), 0)
        < lax.broadcasted_iota(jnp.int32, (edges, edges), 1)
    ).astype(bf16)
    for fetch in fetches:
        fetch.wait()
    h1 = mm(feats[...], w1[...])
    h1 = (h1 / (1.0 + jnp.exp(-h1))).astype(bf16)
    h2 = mm(h1, w2[...])
    h2 = (h2 / (1.0 + jnp.exp(-h2))).astype(bf16)
    w3p = mm(w3[...], perm).astype(bf16)
    vals = mm(h2, w3p)
    lane = lax.broadcasted_iota(jnp.int32, vals.shape, 1)
    vals = jnp.where(lane % LANES == CODE_LANE, code_col[...].astype(f32), vals)
    owner = owner_row[...]
    names = (owner == lax.broadcasted_iota(jnp.int32, (rows, edges), 0)).astype(f32)
    rank = jnp.sum(names * mm(names.astype(bf16), before), axis=0, keepdims=True).astype(jnp.int32)
    target = owner * cap + rank
    place = (target == lax.broadcasted_iota(jnp.int32, (rows * cap, edges), 0)).astype(bf16)
    hi, lo = split2(vals)
    sent = mm(place, hi) + mm(place, lo)
    for g in range(groups):
        part = sent[:, g * LANES : (g + 1) * LANES]
        out[:, g] = part.reshape(rows, cap, LANES)


def own_tiles():
    return [(i, j) for i in range(TILE_DEV) for j in range(TILE_DEV) if abs(i - j) <= HALF]


def tile_at(i, j):
    return i * BAND + j - i + HALF


LOW = [(a, b) for a in range(HALF) for b in range(HALF)]
LOW_PART = [(j, i) for j in range(HALF) for i in range(j - HALF, 0)]
HIGH_PART = [
    (j, i) for j in range(TILE_DEV - HALF, TILE_DEV) for i in range(TILE_DEV, j + HALF + 1)
]
CORNER = len(LOW)
PART = len(LOW_PART)
PAIRS = TILE_DEV // 2


def halo_of(i):
    return [j for j in range(i - HALF, i + HALF + 1) if not 0 <= j < TILE_DEV]


E_CHUNKS = [
    [t for t in own_tiles() if t[0] <= t[1]],
    [(i, j) for i in range(TILE_DEV) for j in halo_of(i)],
]
W_CHUNKS = [
    [
        (i, j)
        for i in (2 * p, 2 * p + 1)
        for j in range(i - HALF, i + HALF + 1)
        if not (0 <= j < i)
    ]
    for p in range(PAIRS)
]
E_AT = {t: n for n, t in enumerate(sum(E_CHUNKS, []))}
W_AT = {t: n for n, t in enumerate(sum(W_CHUNKS, []))}
SENT = len(E_AT)
HALO_SLOT = {t: n for n, t in enumerate(E_CHUNKS[1])}


def band_kernel(
    rows, groups, scale, rec, out,
    dh, rh, le, lw, fe, fw, sp, rp, se, re, sw, rw, bhi, blo, ahi, alo, t1, s_sem, r_sem,
):
    r = lax.axis_index("rows")
    g = lax.axis_index("feat")
    width = TILE // groups
    cols = BLOCK // groups
    up, down = lax.rem(r + 1, rows), lax.rem(r + rows - 1, rows)
    y, c = g // 2, g % 2
    core_peer, y_peer = y * 2 + (1 - c), (1 - y) * 2 + c
    mine = pl.ds(pl.multiple_of(g * width, width), width)
    theirs = pl.ds(pl.multiple_of(y_peer * width, width), width)

    barrier = pltpu.get_barrier_semaphore()
    for who in ((up, g), (down, g), (r, core_peer), (r, y_peer)):
        pl.semaphore_signal(barrier, inc=1, device_id=who, device_id_type=MESH)

    x = rec[...]
    count = x.shape[0]
    code_c = x[:, CODE_LANE : CODE_LANE + 1].astype(jnp.int32)
    code_r = x.T[CODE_LANE : CODE_LANE + 1, :].astype(jnp.int32)
    hi, lo = split2(x)
    lane = lax.broadcasted_iota(jnp.int32, (1, cols * TILE), 1)
    lane_block = lane % width // cols
    tile_id = lax.shift_right_logical(code_r, 10) % 8 * BAND + lax.shift_right_logical(code_r, 3) % 16
    valid = code_r >= 8192
    src_r, dst_r = lax.shift_right_logical(code_r, 7) % 8, code_r % 8
    src_c, dst_c = lax.shift_right_logical(code_c, 7) % 8, code_c % 8
    line = lax.broadcasted_iota(jnp.int32, (NT * NB, count), 0)
    by_col, by_row = spread_columns(groups, cols, g)

    def scatter(dest, spread, row_block, lane_of):
        index = jnp.where(valid, tile_id * NB + row_block, -1)
        place = (line == index).astype(bf16)
        keep = lane_block == lane_of
        strips_hi = jnp.where(keep, mm(hi, spread), 0.0).astype(bf16)
        strips_lo = jnp.where(keep, mm(lo, spread), 0.0).astype(bf16)
        total = mm(place, strips_hi) + mm(place, strips_lo)
        for u in range(cols):
            dest[:, pl.ds(u, NB, stride=cols), :] = total[:, u * TILE : (u + 1) * TILE].reshape(
                NT, NB, TILE
            )

    def copy(src, dst, sem, who):
        return pltpu.make_async_remote_copy(
            src_ref=src, dst_ref=dst, send_sem=s_sem.at[sem], recv_sem=r_sem.at[sem],
            device_id=who, device_id_type=MESH,
        )

    pending = []

    def start(*args):
        item = copy(*args)
        item.start()
        pending.append(item)
        return item

    def gather(buf, first, size, sem):
        part = buf.at[pl.ds(first, size), mine]
        near = start(part, part, sem, (r, core_peer))
        far = start(part, part, sem + 1, (r, y_peer))
        return near, far, buf.at[pl.ds(first, size), theirs], sem + 2

    def forward(item):
        item[1].wait_recv()
        return start(item[2], item[2], item[3], (r, core_peer))

    def put_a(jj, kk, val):
        h, l = split2(val)
        ahi[jj * width : (jj + 1) * width, kk * TILE : (kk + 1) * TILE] = h
        alo[jj * width : (jj + 1) * width, kk * TILE : (kk + 1) * TILE] = l

    def put_b(kk, i, val):
        h, l = split2(val)
        bhi[kk * TILE : (kk + 1) * TILE, i * TILE : (i + 1) * TILE] = h
        blo[kk * TILE : (kk + 1) * TILE, i * TILE : (i + 1) * TILE] = l

    def build_own(buf, rows_of):
        for i in rows_of:
            for s in range(BAND):
                put_a(i + s, i + HALF, buf[i * BAND + s])

    def build_corner(recv, side):
        at = 0 if side == 0 else WIN - HALF
        for n, (a, b) in enumerate(LOW):
            put_a(b + at, a + at, recv[side, n])

    def build_tiles(buf, index, tiles):
        for i, j in tiles:
            full = buf[index[i, j]]
            put_b(j + HALF, i, full)
            if i != j:
                turned = full.T
                if 0 <= j < TILE_DEV:
                    put_b(i + HALF, j, turned)
                else:
                    t1[HALO_SLOT[i, j]] = turned
        for i, j in tiles:
            if not 0 <= j < TILE_DEV:
                put_a(i + HALF, j + HALF, t1[HALO_SLOT[i, j], mine, :])

    def product(p, emit):
        rows_at = slice(2 * p * width, (2 * p + 10) * width)
        mid = slice(2 * p * TILE, (2 * p + 10) * TILE)
        cols_at = slice(2 * p * TILE, (2 * p + 2) * TILE)
        a_h, b_h = ahi[rows_at, mid], bhi[mid, cols_at]
        acc = mm(a_h, b_h) + mm(a_h, blo[mid, cols_at]) + mm(alo[rows_at, mid], b_h)
        for di in range(2):
            for s in range(BAND):
                m = s + di
                emit(2 * p + di, s, acc[m * width : (m + 1) * width, di * TILE : (di + 1) * TILE])

    scatter(rh, by_row, src_r, dst_c)
    for n, (j, i) in enumerate(LOW_PART):
        sp[0, n] = rh[tile_at(j, i)]
    for n, (j, i) in enumerate(HIGH_PART):
        sp[1, n] = rh[tile_at(j, i)]
    pl.semaphore_wait(barrier, 4)
    part_low = start(sp.at[0], rp.at[1], 0, (down, g))
    part_high = start(sp.at[1], rp.at[0], 1, (up, g))
    scatter(dh, by_col, dst_r, src_c)
    for i, j in own_tiles():
        val = scale * (dh[tile_at(i, j)] + rh[tile_at(j, i)])
        le[tile_at(i, j)] = val
        if i <= j:
            fe[E_AT[i, j], mine, :] = val
    first_chunk = gather(fe, 0, len(E_CHUNKS[0]), 2)
    for n, (a, b) in enumerate(LOW):
        se[0, n] = le[tile_at(a, b)]
        se[1, n] = le[tile_at(a + HALF, b + HALF)]
    part_low.wait_recv()
    part_high.wait_recv()
    for n, (j, i) in enumerate(HIGH_PART):
        own, halo = i - TILE_DEV, j - TILE_DEV
        val = scale * (dh[tile_at(own, halo)] + rp[0, n])
        le[tile_at(own, halo)] = val
        fe[E_AT[own, halo], mine, :] = val
    for n, (j, i) in enumerate(LOW_PART):
        own, halo = i + TILE_DEV, j + TILE_DEV
        val = scale * (dh[tile_at(own, halo)] + rp[1, n])
        le[tile_at(own, halo)] = val
        fe[E_AT[own, halo], mine, :] = val
    second_chunk = gather(fe, len(E_CHUNKS[0]), len(E_CHUNKS[1]), 5)
    to_low = start(se.at[0], re.at[1], 8, (down, g))
    to_high = start(se.at[1], re.at[0], 9, (up, g))

    zero_block = jnp.zeros((TILE, TILE), bf16)
    for p in range(PAIRS):
        for i, kk in ((2 * p, 2 * p + 9), (2 * p + 1, 2 * p)):
            for ref in (bhi, blo):
                ref[kk * TILE : (kk + 1) * TILE, i * TILE : (i + 1) * TILE] = zero_block
    ahi[...] = jnp.zeros(ahi.shape, bf16)
    alo[...] = jnp.zeros(alo.shape, bf16)
    build_own(le, range(TILE_DEV))
    on = forward(first_chunk)
    first_chunk[0].wait_recv()
    on.wait_recv()
    build_tiles(fe, E_AT, E_CHUNKS[0])
    on = forward(second_chunk)
    second_chunk[0].wait_recv()
    on.wait_recv()
    build_tiles(fe, E_AT, E_CHUNKS[1])
    to_low.wait_recv()
    to_high.wait_recv()
    for side in range(2):
        build_corner(re, side)

    def first(i, s, acc):
        val = le[i * BAND + s] + acc
        lw[i * BAND + s] = val
        if (i, i + s - HALF) in W_AT:
            fw[W_AT[i, i + s - HALF], mine, :] = val

    chunks = []
    begin = 0
    corners = [None, None]
    for p in range(PAIRS):
        product(p, first)
        chunks.append(gather(fw, begin, len(W_CHUNKS[p]), 10 + 3 * p))
        begin += len(W_CHUNKS[p])
        if p == PAIRS // 2 - 1:
            for n, (a, b) in enumerate(LOW):
                sw[0, n] = lw[tile_at(a, b)]
            corners[1] = start(sw.at[0], rw.at[1], 22, (down, g))
    for n, (a, b) in enumerate(LOW):
        sw[1, n] = lw[tile_at(a + HALF, b + HALF)]
    corners[0] = start(sw.at[1], rw.at[0], 23, (up, g))
    build_own(lw, range(TILE_DEV))
    eye = (
        lax.broadcasted_iota(jnp.int32, (width, TILE), 0) + g * width
        == lax.broadcasted_iota(jnp.int32, (width, TILE), 1)
    ).astype(f32)

    def second(i, s, acc):
        val = 1.5 * lw[i * BAND + s] - acc
        if s == HALF:
            val = val + 0.4375 * eye
        out[i, s] = val

    for half in range(2):
        for p in (2 * half, 2 * half + 1):
            on = forward(chunks[p])
            chunks[p][0].wait_recv()
            on.wait_recv()
            build_tiles(fw, W_AT, W_CHUNKS[p])
        corners[half].wait_recv()
        build_corner(rw, half)
        for p in (2 * half, 2 * half + 1):
            product(p, second)
    for item in pending:
        item.wait_send()


def local(edge_feats, edge_owner, src_local, band_slot, dst_local, w_first, w_second, w_third):
    groups = lax.axis_size("feat")
    rows = lax.axis_size("rows")
    edges = edge_feats.shape[0]
    cap = max(2, 2 * edges // rows)
    width = TILE // groups
    code = 8192 + src_local * 128 + band_slot * 8 + dst_local
    vm = pl.BlockSpec(memory_space=pltpu.VMEM)
    operands = (
        edge_feats, edge_owner.reshape(1, edges), code.reshape(edges, 1), w_first, w_second, w_third,
    )
    sent = pl.pallas_call(
        functools.partial(route_kernel, rows, cap, groups),
        out_shape=jax.ShapeDtypeStruct((rows, groups, cap, LANES), f32),
        in_specs=[pl.BlockSpec(memory_space=pl.ANY)] * 6,
        out_specs=vm,
        scratch_shapes=[pltpu.VMEM(item.shape, item.dtype) for item in operands]
        + [pltpu.SemaphoreType.DMA((6,))],
        compiler_params=pltpu.CompilerParams(vmem_limit_bytes=56 << 20),
    )(*operands)
    sent = sent.reshape(rows * groups, cap, LANES)
    got = lax.all_to_all(sent, ("rows", "feat"), 0, 0, tiled=True)
    rec = got.reshape(rows * groups * cap, LANES)
    degree = groups * edges / (TILE_DEV * NB)
    scale = 0.5 * (0.5 / math.sqrt(2.0 * BLOCK * degree))
    tiles = (NT, width, TILE)
    return pl.pallas_call(
        functools.partial(band_kernel, rows, groups, scale),
        out_shape=jax.ShapeDtypeStruct((TILE_DEV, BAND, width, TILE), f32),
        in_specs=[vm],
        out_specs=vm,
        scratch_shapes=[pltpu.VMEM(tiles, f32)] * 4
        + [pltpu.VMEM((SENT, TILE, TILE), f32)] * 2
        + [pltpu.VMEM((2, PART, width, TILE), f32)] * 2
        + [pltpu.VMEM((2, CORNER, width, TILE), f32)] * 4
        + [pltpu.VMEM((WIN * TILE, TILE_DEV * TILE), bf16)] * 2
        + [pltpu.VMEM((WIN * width, WIN * TILE), bf16)] * 2
        + [pltpu.VMEM((len(HALO_SLOT), TILE, TILE), f32)]
        + [pltpu.SemaphoreType.DMA((24,))] * 2,
        compiler_params=pltpu.CompilerParams(
            collective_id=0, has_side_effects=True, vmem_limit_bytes=60 << 20
        ),
    )(rec)


def solution(mesh):
    in_specs = (
        P(("rows", "feat"), None),
        P(("rows", "feat"), None),
        P(("rows", "feat")),
        P(("rows", "feat")),
        P(("rows", "feat")),
        P(),
        P(),
        P(),
    )
    out_specs = P("rows", None, "feat", None)
    return jax.shard_map(local, mesh=mesh, in_specs=in_specs, out_specs=out_specs, check_vma=False)
```

time: 144 us -> 96.9 us (0.67)
  Pallas kernels: 102 us -> 59.8 us
  blocking collectives: 0 us -> 31.7 us
  waiting for transfers between devices: 23.7 us -> 0 us
  local copies, waits for them, and re-layouts: 10.3 us -> 3.15 us
  starting transfers between devices: 6.36 us -> 0 us
    pallas_call x1, Pallas kernels: 99.8 us -> 56.6 us  [local(): pl.pallas_call(functools.partial(band_kernel, rows, groups, scale), out_s...]
    all_to_all x0 -> x1, blocking collectives: none -> 31.7 us  [local(): got = lax.all_to_all(sent, ('rows', 'feat'), 0, 0, tiled=True)]
    all_to_all x1 -> x0, waiting for transfers between devices: 23.7 us -> none  [local(): got = lax.all_to_all(sent, ('rows', 'feat'), 0, 0, tiled=True)]
    all_to_all x1 -> x0, starting transfers between devices: 6.36 us -> none  [local(): got = lax.all_to_all(sent, ('rows', 'feat'), 0, 0, tiled=True)]
    unnamed x15 -> x1, local copies, waits for them, and re-layouts: 8.58 us -> 2.36 us
    squeeze x1 -> x0, local copies, waits for them, and re-layouts: 1.58 us -> none  [local(): by_row = jnp.asarray(by_row, bf16)[lax.axis_index('feat')]]
  transfers between devices with their start and end apart: 1 -> 0, of which waited for: 1 -> 0; matrix products, arithmetic and copies ran while one was open for 1% -> 0% of each run, Pallas kernels for 0% -> 0%
where the time goes in v2:
time: 96.9 us; the launch traced here: 95.4 us
  Pallas kernels  59.8 us (62%)
  blocking collectives  31.7 us (33%)
  local copies, waits for them, and re-layouts  3.15 us (3%)
    pallas_call x1, Pallas kernels, local(): pl.pallas_call(functools.partial(band_kernel, rows, groups, scale), out_s...  56.6 us
    all_to_all x1, blocking collectives, local(): got = lax.all_to_all(sent, ('rows', 'feat'), 0, 0, tiled=True)  31.7 us
    pallas_call x1, Pallas kernels, local(): pl.pallas_call(functools.partial(route_kernel, rows, cap, groups), out_sh...  3.18 us
    unnamed x1, local copies, waits for them, and re-layouts  2.36 us

profile of v2, /device:TPU:9, one launch (start us, length us, event | category | flops | bytes accessed | tf_op | source)
XLA Modules:
  0.0 95.4 jit_solution(2660367066394326568)
XLA Ops:
  0.0 0.7 add_add_fusion
  0.7 0.8 copy.9.code_in
  1.5 3.2 %shard_map.82 = f32[8,4,64,128]{3,2,1,0:T(8,128)} custom-call(bf16[256,256]{1,0:T(8,128)(2,1)} %feats_in.1, s32[1,256]{1,0:T(1,128)} %bitcast.7, s32[256,1]{1,0:T(8,128)} %copy.9.code_in, bf16[256,256]{1,0:T(8,128)(2,1)} %w1_in.1, bf16[256,256]{1,0:T(8,128)(2,1)} %w2_in.1, bf16[256,256]{1,0:T(8,128)(2,1)} %w3_in.1), custom_call_target="tpu_custom_call" | custom-call | tf_op jit(solution)/shard_map/pallas_call | solution.py:369
  4.7 31.7 %all_to_all.5 = f32[32,64,128]{2,1,0:T(8,128)} all-to-all(f32[32,64,128]{2,1,0:T(8,128)} %bitcast.4), channel_id=1, replica_groups=mesh['rows'=8,'feat'=4] {'rows','feat'}, dimensions={0} | all-to-all | bytes 2097152 | tf_op jit(solution)/shard_map/all_to_all | solution.py:379
  36.4 56.6 %shard_map.83 = f32[8,9,32,128]{3,2,1,0:T(8,128)} custom-call(f32[2048,128]{1,0:T(8,128)} %bitcast.5), custom_call_target="tpu_custom_call" | custom-call | tf_op jit(solution)/shard_map/pallas_call | solution.py:384
  93.1 2.4 %copy.11 = f32[8,9,32,128]{3,2,1,0:T(8,128)} copy(f32[8,9,32,128]{3,2,1,0:T(8,128)} %shard_map.83) | data formatting | bytes 2359296

commit v3 on v2

--- a/solution.py
+++ b/solution.py
@@ -62,18 +62,50 @@
 
 
 def route_kernel(
-    rows, cap, groups, feats_in, owner_in, code_in, w1_in, w2_in, w3_in, out,
-    feats, owner_row, code_col, w1, w2, w3, sems,
+    rows, cap, groups,
+    feats_in, owner_in, src_in, slot_in, dst_in, w1_in, w2_in, w3_in, dh, rh,
+    feats, owner_row, src_row, slot_row, dst_row, w1, w2, w3, sent, rec, acc_col, acc_row,
+    sems, s_sem, r_sem,
 ):
+    r = lax.axis_index("rows")
+    g = lax.axis_index("feat")
+    n = rows * groups
+    edges = feats.shape[0]
+    cols = BLOCK // groups
+    width = TILE // groups
+
+    def partner(q):
+        turn = q // groups
+        step = rows // 2 + (turn + 1) // 2 * (1 - 2 * (turn % 2))
+        return (r + step + rows) % rows, (g + groups - 1 - q % groups) % groups
+
+    def record_copy(q):
+        to_row, to_group = partner(q)
+        return pltpu.make_async_remote_copy(
+            src_ref=sent.at[to_row, to_group], dst_ref=rec.at[q],
+            send_sem=s_sem.at[q], recv_sem=r_sem.at[q],
+            device_id=(to_row, to_group), device_id_type=MESH,
+        )
+
+    barrier = pltpu.get_barrier_semaphore()
+
+    def greet(q, carry):
+        pl.semaphore_signal(barrier, inc=1, device_id=partner(q), device_id_type=MESH)
+        return carry
+
+    lax.fori_loop(0, n - 1, greet, 0)
+
     fetches = []
-    for n, (src, dst) in enumerate(
-        ((feats_in, feats), (w1_in, w1), (w2_in, w2), (w3_in, w3), (owner_in, owner_row), (code_in, code_col))
+    for k, (src, dst) in enumerate(
+        (
+            (feats_in, feats), (w1_in, w1), (w2_in, w2), (w3_in, w3), (owner_in, owner_row),
+            (src_in, src_row), (slot_in, slot_row), (dst_in, dst_row),
+        )
     ):
-        fetch = pltpu.make_async_copy(src, dst, sems.at[n])
+        fetch = pltpu.make_async_copy(src, dst, sems.at[k])
         fetch.start()
         fetches.append(fetch)
-    edges = feats.shape[0]
-    perm = piece_columns(groups, BLOCK // groups)
+    perm = piece_columns(groups, cols)
     before = (
         lax.broadcasted_iota(jnp.int32, (edges, edges), 0)
         < lax.broadcasted_iota(jnp.int32, (edges, edges), 1)
@@ -86,18 +118,78 @@
     h2 = (h2 / (1.0 + jnp.exp(-h2))).astype(bf16)
     w3p = mm(w3[...], perm).astype(bf16)
     vals = mm(h2, w3p)
+    code = (8192 + src_row[...] * 128 + slot_row[...] * 8 + dst_row[...]).astype(f32)
+    code_col = jnp.broadcast_to(code, (LANES, edges)).T[:, :1]
     lane = lax.broadcasted_iota(jnp.int32, vals.shape, 1)
-    vals = jnp.where(lane % LANES == CODE_LANE, code_col[...].astype(f32), vals)
+    vals = jnp.where(lane % LANES == CODE_LANE, code_col, vals)
     owner = owner_row[...]
     names = (owner == lax.broadcasted_iota(jnp.int32, (rows, edges), 0)).astype(f32)
     rank = jnp.sum(names * mm(names.astype(bf16), before), axis=0, keepdims=True).astype(jnp.int32)
     target = owner * cap + rank
     place = (target == lax.broadcasted_iota(jnp.int32, (rows * cap, edges), 0)).astype(bf16)
     hi, lo = split2(vals)
-    sent = mm(place, hi) + mm(place, lo)
-    for g in range(groups):
-        part = sent[:, g * LANES : (g + 1) * LANES]
-        out[:, g] = part.reshape(rows, cap, LANES)
+    packed = mm(place, hi) + mm(place, lo)
+    for k in range(groups):
+        part = packed[:, k * LANES : (k + 1) * LANES]
+        sent[:, k] = part.reshape(rows, cap, LANES)
+
+    pl.semaphore_wait(barrier, n - 1)
+
+    def send(q, carry):
+        record_copy(q).start()
+        return carry
+
+    lax.fori_loop(0, n - 1, send, 0)
+    rec[n - 1] = sent[r, g]
+
+    by_col, by_row = spread_columns(groups, cols, g)
+    spread_lane = lax.broadcasted_iota(jnp.int32, (1, cols * TILE), 1)
+    lane_block = spread_lane % width // cols
+    shares = 4
+    size = n // shares
+    line = lax.broadcasted_iota(jnp.int32, (NT * NB, size * cap), 0)
+
+    def arrived(q, carry):
+        record_copy(q).wait_recv()
+        return carry
+
+    for share in reversed(range(shares)):
+        lax.fori_loop(share * size, min((share + 1) * size, n - 1), arrived, 0)
+        x = rec[share * size : (share + 1) * size].reshape(size * cap, LANES)
+        code_c = x[:, CODE_LANE : CODE_LANE + 1].astype(jnp.int32)
+        code_r = x.T[CODE_LANE : CODE_LANE + 1, :].astype(jnp.int32)
+        hi, lo = split2(x)
+        tile_id = (
+            lax.shift_right_logical(code_r, 10) % 8 * BAND + lax.shift_right_logical(code_r, 3) % 16
+        )
+        valid = code_r >= 8192
+        src_r, dst_r = lax.shift_right_logical(code_r, 7) % 8, code_r % 8
+        src_c, dst_c = lax.shift_right_logical(code_c, 7) % 8, code_c % 8
+        for acc, spread, row_block, lane_of in (
+            (acc_row, by_row, src_r, dst_c),
+            (acc_col, by_col, dst_r, src_c),
+        ):
+            index = jnp.where(valid, tile_id * NB + row_block, -1)
+            put = (line == index).astype(bf16)
+            keep = lane_block == lane_of
+            strips_hi = jnp.where(keep, mm(hi, spread), 0.0).astype(bf16)
+            strips_lo = jnp.where(keep, mm(lo, spread), 0.0).astype(bf16)
+            total = mm(put, strips_hi) + mm(put, strips_lo)
+            if share == shares - 1:
+                acc[...] = total
+            else:
+                acc[...] += total
+    for dest, acc in ((rh, acc_row), (dh, acc_col)):
+        for u in range(cols):
+            dest[:, pl.ds(u, NB, stride=cols), :] = acc[:, u * TILE : (u + 1) * TILE].reshape(
+                NT, NB, TILE
+            )
+
+    def sent_off(q, carry):
+        record_copy(q).wait_send()
+        return carry
+
+    lax.fori_loop(0, n - 1, sent_off, 0)
 
 
 def own_tiles():
@@ -142,13 +234,12 @@
 
 
 def band_kernel(
-    rows, groups, scale, rec, out,
-    dh, rh, le, lw, fe, fw, sp, rp, se, re, sw, rw, bhi, blo, ahi, alo, t1, s_sem, r_sem,
+    rows, groups, scale, dh_in, rh_in, out,
+    dh, rh, le, lw, fe, fw, sp, rp, se, re, sw, rw, bhi, blo, ahi, alo, t1, sems, s_sem, r_sem,
 ):
     r = lax.axis_index("rows")
     g = lax.axis_index("feat")
     width = TILE // groups
-    cols = BLOCK // groups
     up, down = lax.rem(r + 1, rows), lax.rem(r + rows - 1, rows)
     y, c = g // 2, g % 2
     core_peer, y_peer = y * 2 + (1 - c), (1 - y) * 2 + c
@@ -159,31 +250,10 @@
     for who in ((up, g), (down, g), (r, core_peer), (r, y_peer)):
         pl.semaphore_signal(barrier, inc=1, device_id=who, device_id_type=MESH)
 
-    x = rec[...]
-    count = x.shape[0]
-    code_c = x[:, CODE_LANE : CODE_LANE + 1].astype(jnp.int32)
-    code_r = x.T[CODE_LANE : CODE_LANE + 1, :].astype(jnp.int32)
-    hi, lo = split2(x)
-    lane = lax.broadcasted_iota(jnp.int32, (1, cols * TILE), 1)
-    lane_block = lane % width // cols
-    tile_id = lax.shift_right_logical(code_r, 10) % 8 * BAND + lax.shift_right_logical(code_r, 3) % 16
-    valid = code_r >= 8192
-    src_r, dst_r = lax.shift_right_logical(code_r, 7) % 8, code_r % 8
-    src_c, dst_c = lax.shift_right_logical(code_c, 7) % 8, code_c % 8
-    line = lax.broadcasted_iota(jnp.int32, (NT * NB, count), 0)
-    by_col, by_row = spread_columns(groups, cols, g)
-
-    def scatter(dest, spread, row_block, lane_of):
-        index = jnp.where(valid, tile_id * NB + row_block, -1)
-        place = (line == index).astype(bf16)
-        keep = lane_block == lane_of
-        strips_hi = jnp.where(keep, mm(hi, spread), 0.0).astype(bf16)
-        strips_lo = jnp.where(keep, mm(lo, spread), 0.0).astype(bf16)
-        total = mm(place, strips_hi) + mm(place, strips_lo)
-        for u in range(cols):
-            dest[:, pl.ds(u, NB, stride=cols), :] = total[:, u * TILE : (u + 1) * TILE].reshape(
-                NT, NB, TILE
-            )
+    rh_fetch = pltpu.make_async_copy(rh_in, rh, sems.at[0])
+    dh_fetch = pltpu.make_async_copy(dh_in, dh, sems.at[1])
+    rh_fetch.start()
+    dh_fetch.start()
 
     def copy(src, dst, sem, who):
         return pltpu.make_async_remote_copy(
@@ -254,7 +324,7 @@
                 m = s + di
                 emit(2 * p + di, s, acc[m * width : (m + 1) * width, di * TILE : (di + 1) * TILE])
 
-    scatter(rh, by_row, src_r, dst_c)
+    rh_fetch.wait()
     for n, (j, i) in enumerate(LOW_PART):
         sp[0, n] = rh[tile_at(j, i)]
     for n, (j, i) in enumerate(HIGH_PART):
@@ -262,7 +332,7 @@
     pl.semaphore_wait(barrier, 4)
     part_low = start(sp.at[0], rp.at[1], 0, (down, g))
     part_high = start(sp.at[1], rp.at[0], 1, (up, g))
-    scatter(dh, by_col, dst_r, src_c)
+    dh_fetch.wait()
     for i, j in own_tiles():
         val = scale * (dh[tile_at(i, j)] + rh[tile_at(j, i)])
         le[tile_at(i, j)] = val
@@ -361,30 +431,40 @@
     edges = edge_feats.shape[0]
     cap = max(2, 2 * edges // rows)
     width = TILE // groups
-    code = 8192 + src_local * 128 + band_slot * 8 + dst_local
+    tiles = (NT, width, TILE)
     vm = pl.BlockSpec(memory_space=pltpu.VMEM)
+    anywhere = pl.BlockSpec(memory_space=pl.ANY)
     operands = (
-        edge_feats, edge_owner.reshape(1, edges), code.reshape(edges, 1), w_first, w_second, w_third,
+        edge_feats, edge_owner.reshape(1, edges), src_local.reshape(1, edges),
+        band_slot.reshape(1, edges), dst_local.reshape(1, edges), w_first, w_second, w_third,
     )
-    sent = pl.pallas_call(
+    partners = rows * groups
+    sums = pltpu.VMEM((NT * NB, BLOCK // groups * TILE), f32)
+    by_col, by_row = pl.pallas_call(
         functools.partial(route_kernel, rows, cap, groups),
-        out_shape=jax.ShapeDtypeStruct((rows, groups, cap, LANES), f32),
-        in_specs=[pl.BlockSpec(memory_space=pl.ANY)] * 6,
-        out_specs=vm,
+        out_shape=[jax.ShapeDtypeStruct(tiles, f32)] * 2,
+        in_specs=[anywhere] * len(operands),
+        out_specs=[vm] * 2,
         scratch_shapes=[pltpu.VMEM(item.shape, item.dtype) for item in operands]
-        + [pltpu.SemaphoreType.DMA((6,))],
-        compiler_params=pltpu.CompilerParams(vmem_limit_bytes=56 << 20),
+        + [
+            pltpu.VMEM((rows, groups, cap, LANES), f32),
+            pltpu.VMEM((partners, cap, LANES), f32),
+            sums,
+            sums,
+            pltpu.SemaphoreType.DMA((len(operands),)),
+            pltpu.SemaphoreType.DMA((partners,)),
+            pltpu.SemaphoreType.DMA((partners,)),
+        ],
+        compiler_params=pltpu.CompilerParams(
+            collective_id=0, has_side_effects=True, vmem_limit_bytes=56 << 20
+        ),
     )(*operands)
-    sent = sent.reshape(rows * groups, cap, LANES)
-    got = lax.all_to_all(sent, ("rows", "feat"), 0, 0, tiled=True)
-    rec = got.reshape(rows * groups * cap, LANES)
     degree = groups * edges / (TILE_DEV * NB)
     scale = 0.5 * (0.5 / math.sqrt(2.0 * BLOCK * degree))
-    tiles = (NT, width, TILE)
     return pl.pallas_call(
         functools.partial(band_kernel, rows, groups, scale),
         out_shape=jax.ShapeDtypeStruct((TILE_DEV, BAND, width, TILE), f32),
-        in_specs=[vm],
+        in_specs=[anywhere] * 2,
         out_specs=vm,
         scratch_shapes=[pltpu.VMEM(tiles, f32)] * 4
         + [pltpu.VMEM((SENT, TILE, TILE), f32)] * 2
@@ -393,11 +473,12 @@
         + [pltpu.VMEM((WIN * TILE, TILE_DEV * TILE), bf16)] * 2
         + [pltpu.VMEM((WIN * width, WIN * TILE), bf16)] * 2
         + [pltpu.VMEM((len(HALO_SLOT), TILE, TILE), f32)]
+        + [pltpu.SemaphoreType.DMA((2,))]
         + [pltpu.SemaphoreType.DMA((24,))] * 2,
         compiler_params=pltpu.CompilerParams(
-            collective_id=0, has_side_effects=True, vmem_limit_bytes=60 << 20
+            collective_id=1, has_side_effects=True, vmem_limit_bytes=60 << 20
         ),
-    )(rec)
+    )(by_col, by_row)
 
 
 def solution(mesh):

time: 96.9 us -> 92.1 us (0.950); the launches traced: 95.4 us -> 91.9 us
  blocking collectives: 31.7 us -> 0 us
  Pallas kernels: 59.8 us -> 89.6 us
    all_to_all x1 -> x0, blocking collectives: 31.7 us -> none  [local(): got = lax.all_to_all(sent, ('rows', 'feat'), 0, 0, tiled=True)]
    pallas_call x1, Pallas kernels: 3.18 us -> 34.8 us  [local(): pl.pallas_call(functools.partial(route_kernel, rows, cap, groups), out_sh...]
    pallas_call x1, Pallas kernels: 56.6 us -> 54.8 us  [local(): pl.pallas_call(functools.partial(band_kernel, rows, groups, scale), out_s...]
where the time goes in v3:
time: 92.1 us; the launch traced here: 91.9 us
  Pallas kernels  89.6 us (97%)
  local copies, waits for them, and re-layouts  2.36 us (3%)
    pallas_call x1, Pallas kernels, local(): pl.pallas_call(functools.partial(band_kernel, rows, groups, scale), out_s...  54.8 us
    pallas_call x1, Pallas kernels, local(): pl.pallas_call(functools.partial(route_kernel, rows, cap, groups), out_sh...  34.8 us
    unnamed x1, local copies, waits for them, and re-layouts  2.36 us

profile of v3, /device:TPU:9, one launch (start us, length us, event | category | flops | bytes accessed | tf_op | source)
XLA Modules:
  0.0 91.9 jit_solution(6125350910100733013)
XLA Ops:
  0.0 34.8 %shard_map.82 = (f32[72,32,128]{2,1,0:T(8,128)}, f32[72,32,128]{2,1,0:T(8,128)}) custom-call(bf16[256,256]{1,0:T(8,128)(2,1)} %feats_in.1, s32[1,256]{1,0:T(1,128)} %bitcast.4, s32[1,256]{1,0:T(1,128)} %bitcast.5, s32[1,256]{1,0:T(1,128)} %bitcast.6, s32[1,256]{1,0:T(1,128)} %bitcast.7, bf16[256,256]{1,0:T(8,128)(2,1)} %w1_in.1, bf16[256,256]{1,0:T(8,128)(2,1)} %w2_in.1, ...), custom_call_target="tpu_custom_call" | custom-call | tf_op jit(solution)/shard_map/pallas_call | solution.py:443
  34.8 54.8 %shard_map.83 = f32[8,9,32,128]{3,2,1,0:T(8,128)} custom-call(f32[72,32,128]{2,1,0:T(8,128)} %get-tuple-element.7.dh_in, f32[72,32,128]{2,1,0:T(8,128)} %get-tuple-element.8.rh_in), custom_call_target="tpu_custom_call" | custom-call | tf_op jit(solution)/shard_map/pallas_call | solution.py:464
  89.6 2.4 %copy.10 = f32[8,9,32,128]{3,2,1,0:T(8,128)} copy(f32[8,9,32,128]{3,2,1,0:T(8,128)} %shard_map.83) | data formatting | bytes 2359296

commit v4 on v3

--- a/solution.py
+++ b/solution.py
@@ -218,24 +218,18 @@
     [t for t in own_tiles() if t[0] <= t[1]],
     [(i, j) for i in range(TILE_DEV) for j in halo_of(i)],
 ]
-W_CHUNKS = [
-    [
-        (i, j)
-        for i in (2 * p, 2 * p + 1)
-        for j in range(i - HALF, i + HALF + 1)
-        if not (0 <= j < i)
-    ]
-    for p in range(PAIRS)
-]
 E_AT = {t: n for n, t in enumerate(sum(E_CHUNKS, []))}
-W_AT = {t: n for n, t in enumerate(sum(W_CHUNKS, []))}
 SENT = len(E_AT)
+OWN = len(E_CHUNKS[0])
+SIDE = len(E_CHUNKS[1]) // 2
+SIDES = [E_CHUNKS[1][:SIDE], E_CHUNKS[1][SIDE:]]
 HALO_SLOT = {t: n for n, t in enumerate(E_CHUNKS[1])}
+OWN_SLOT = {t: n for n, t in enumerate(t for t in E_CHUNKS[0] if t[0] != t[1])}
 
 
 def band_kernel(
     rows, groups, scale, dh_in, rh_in, out,
-    dh, rh, le, lw, fe, fw, sp, rp, se, re, sw, rw, bhi, blo, ahi, alo, t1, sems, s_sem, r_sem,
+    dh, rh, le, lw, fe, fw, sp, rp, se, re, sw, rw, bhi, blo, fhi, flo, ahi, alo, t1, tw, sems, s_sem, r_sem,
 ):
     r = lax.axis_index("rows")
     g = lax.axis_index("feat")
@@ -284,41 +278,92 @@
         ahi[jj * width : (jj + 1) * width, kk * TILE : (kk + 1) * TILE] = h
         alo[jj * width : (jj + 1) * width, kk * TILE : (kk + 1) * TILE] = l
 
-    def put_b(kk, i, val):
-        h, l = split2(val)
-        bhi[kk * TILE : (kk + 1) * TILE, i * TILE : (i + 1) * TILE] = h
-        blo[kk * TILE : (kk + 1) * TILE, i * TILE : (i + 1) * TILE] = l
-
-    def build_own(buf, rows_of):
-        for i in rows_of:
-            for s in range(BAND):
-                put_a(i + s, i + HALF, buf[i * BAND + s])
+    def put(refs, row, col, parts):
+        for ref, part in zip(refs, parts):
+            ref[row * TILE : (row + 1) * TILE, col * TILE : (col + 1) * TILE] = part
+
+    right, left = (bhi, blo), (fhi, flo)
 
     def build_corner(recv, side):
         at = 0 if side == 0 else WIN - HALF
         for n, (a, b) in enumerate(LOW):
             put_a(b + at, a + at, recv[side, n])
 
-    def build_tiles(buf, index, tiles):
+    def build_start(tiles):
         for i, j in tiles:
-            full = buf[index[i, j]]
-            put_b(j + HALF, i, full)
+            full = fe[E_AT[i, j]]
+            parts = split2(full)
+            put(right, j + HALF, i, parts)
+            inside = 0 <= j < TILE_DEV
+            if inside:
+                put(left, j, i + HALF, parts)
             if i != j:
-                turned = full.T
-                if 0 <= j < TILE_DEV:
-                    put_b(i + HALF, j, turned)
-                else:
-                    t1[HALO_SLOT[i, j]] = turned
+                turned = split2(full.T)
+                put(left, i, j + HALF, turned)
+                if inside:
+                    put(right, i + HALF, j, turned)
+
+    def build_own_square():
+        for i, j in E_CHUNKS[0]:
+            put(right, j + HALF, i, split2(fw[E_AT[i, j]]))
+            if i != j:
+                put(right, i + HALF, j, split2(tw[OWN_SLOT[i, j]]))
+
+    def build_side(tiles):
         for i, j in tiles:
-            if not 0 <= j < TILE_DEV:
-                put_a(i + HALF, j + HALF, t1[HALO_SLOT[i, j], mine, :])
+            full = fw[E_AT[i, j]]
+            put(right, j + HALF, i, split2(full))
+            t1[HALO_SLOT[i, j]] = full.T
+        for i, j in tiles:
+            put_a(i + HALF, j + HALF, t1[HALO_SLOT[i, j], mine, :])
+
+    def three(ref_l, at_l, ref_r, at_r):
+        a_h, b_h = ref_l[0][at_l], ref_r[0][at_r]
+        return mm(a_h, b_h) + mm(a_h, ref_r[1][at_r]) + mm(ref_l[1][at_l], b_h)
+
+    def square(p, q):
+        mid = slice(2 * q * TILE, (2 * p + 10) * TILE)
+        acc = three(
+            left, (slice(2 * q * TILE, (2 * q + 2) * TILE), mid),
+            right, (mid, slice(2 * p * TILE, (2 * p + 2) * TILE)),
+        )
+        for di in range(2):
+            for dj in range(2):
+                i, j = 2 * p + di, 2 * q + dj
+                if (i, j) in E_AT:
+                    n = E_AT[i, j]
+                    val = fe[n] + acc[dj * TILE : (dj + 1) * TILE, di * TILE : (di + 1) * TILE]
+                    fw[n] = val
+                    if i != j:
+                        tw[OWN_SLOT[i, j]] = val.T
+
+    def own_parts(tiles):
+        for i, j in tiles:
+            lw[tile_at(i, j)] = fw[E_AT[i, j], mine, :]
+            if i != j:
+                lw[tile_at(j, i)] = tw[OWN_SLOT[i, j], mine, :]
+
+    def halo_side(side):
+        jj0 = 0 if side == 0 else WIN - HALF
+        mid = slice(0, TILE_DEV * TILE) if side == 0 else slice(TILE_DEV * TILE, WIN * TILE)
+        i0 = 0 if side == 0 else TILE_DEV - HALF
+        acc = three(
+            (ahi, alo), (slice(jj0 * width, (jj0 + HALF) * width), mid),
+            right, (mid, slice(i0 * TILE, (i0 + HALF) * TILE)),
+        )
+        for i, j in SIDES[side]:
+            m = j + HALF - jj0
+            val = le[tile_at(i, j)] + acc[
+                m * width : (m + 1) * width, (i - i0) * TILE : (i - i0 + 1) * TILE
+            ]
+            lw[tile_at(i, j)] = val
+            fw[E_AT[i, j], mine, :] = val
 
     def product(p, emit):
         rows_at = slice(2 * p * width, (2 * p + 10) * width)
         mid = slice(2 * p * TILE, (2 * p + 10) * TILE)
         cols_at = slice(2 * p * TILE, (2 * p + 2) * TILE)
-        a_h, b_h = ahi[rows_at, mid], bhi[mid, cols_at]
-        acc = mm(a_h, b_h) + mm(a_h, blo[mid, cols_at]) + mm(alo[rows_at, mid], b_h)
+        acc = three((ahi, alo), (rows_at, mid), right, (mid, cols_at))
         for di in range(2):
             for s in range(BAND):
                 m = s + di
@@ -359,47 +404,59 @@
     to_high = start(se.at[1], re.at[0], 9, (up, g))
 
     zero_block = jnp.zeros((TILE, TILE), bf16)
+    empty = set()
     for p in range(PAIRS):
-        for i, kk in ((2 * p, 2 * p + 9), (2 * p + 1, 2 * p)):
-            for ref in (bhi, blo):
-                ref[kk * TILE : (kk + 1) * TILE, i * TILE : (i + 1) * TILE] = zero_block
+        empty |= {(2 * p + 9, 2 * p), (2 * p, 2 * p + 1)}
+    for i in range(HALF):
+        empty |= {(kk, i) for kk in range(i)}
+        empty |= {(kk, i + HALF) for kk in range(i + HALF + BAND, WIN)}
+    for kk, i in sorted(empty):
+        put(right, kk, i, (zero_block, zero_block))
+    for p in range(PAIRS):
+        put(left, 2 * p, 2 * p + 9, (zero_block, zero_block))
+        put(left, 2 * p + 1, 2 * p, (zero_block, zero_block))
     ahi[...] = jnp.zeros(ahi.shape, bf16)
     alo[...] = jnp.zeros(alo.shape, bf16)
-    build_own(le, range(TILE_DEV))
+    for i in range(TILE_DEV):
+        for j in halo_of(i):
+            put_a(j + HALF, i + HALF, le[tile_at(i, j)])
     on = forward(first_chunk)
     first_chunk[0].wait_recv()
     on.wait_recv()
-    build_tiles(fe, E_AT, E_CHUNKS[0])
+    build_start(E_CHUNKS[0])
+    for p, q in ((0, 2), (1, 2), (1, 3)):
+        square(p, q)
     on = forward(second_chunk)
     second_chunk[0].wait_recv()
     on.wait_recv()
-    build_tiles(fe, E_AT, E_CHUNKS[1])
-    to_low.wait_recv()
-    to_high.wait_recv()
-    for side in range(2):
-        build_corner(re, side)
-
-    def first(i, s, acc):
-        val = le[i * BAND + s] + acc
-        lw[i * BAND + s] = val
-        if (i, i + s - HALF) in W_AT:
-            fw[W_AT[i, i + s - HALF], mine, :] = val
-
-    chunks = []
-    begin = 0
+    build_start(E_CHUNKS[1])
+
     corners = [None, None]
-    for p in range(PAIRS):
-        product(p, first)
-        chunks.append(gather(fw, begin, len(W_CHUNKS[p]), 10 + 3 * p))
-        begin += len(W_CHUNKS[p])
-        if p == PAIRS // 2 - 1:
-            for n, (a, b) in enumerate(LOW):
-                sw[0, n] = lw[tile_at(a, b)]
-            corners[1] = start(sw.at[0], rw.at[1], 22, (down, g))
+    for p, q in ((0, 0), (0, 1), (1, 1)):
+        square(p, q)
+    own_parts([t for t in E_CHUNKS[0] if t[1] < HALF])
+    for n, (a, b) in enumerate(LOW):
+        sw[0, n] = lw[tile_at(a, b)]
+    corners[1] = start(sw.at[0], rw.at[1], 13, (down, g))
+    for p, q in ((2, 2), (2, 3), (3, 3)):
+        square(p, q)
+    own_parts([t for t in E_CHUNKS[0] if t[0] >= HALF])
     for n, (a, b) in enumerate(LOW):
         sw[1, n] = lw[tile_at(a + HALF, b + HALF)]
-    corners[0] = start(sw.at[1], rw.at[0], 23, (up, g))
-    build_own(lw, range(TILE_DEV))
+    corners[0] = start(sw.at[1], rw.at[0], 14, (up, g))
+    own_parts([t for t in E_CHUNKS[0] if t[0] < HALF <= t[1]])
+
+    chunks = []
+    halos = (to_high, to_low)
+    for side in range(2):
+        halos[side].wait_recv()
+        build_corner(re, side)
+        halo_side(side)
+        chunks.append(gather(fw, OWN + side * SIDE, SIDE, (10, 15)[side]))
+    build_own_square()
+    for i in range(TILE_DEV):
+        for s in range(BAND):
+            put_a(i + s, i + HALF, lw[i * BAND + s])
     eye = (
         lax.broadcasted_iota(jnp.int32, (width, TILE), 0) + g * width
         == lax.broadcasted_iota(jnp.int32, (width, TILE), 1)
@@ -412,11 +469,10 @@
         out[i, s] = val
 
     for half in range(2):
-        for p in (2 * half, 2 * half + 1):
-            on = forward(chunks[p])
-            chunks[p][0].wait_recv()
-            on.wait_recv()
-            build_tiles(fw, W_AT, W_CHUNKS[p])
+        on = forward(chunks[half])
+        chunks[half][0].wait_recv()
+        on.wait_recv()
+        build_side(SIDES[half])
         corners[half].wait_recv()
         build_corner(rw, half)
         for p in (2 * half, 2 * half + 1):
@@ -471,10 +527,12 @@
         + [pltpu.VMEM((2, PART, width, TILE), f32)] * 2
         + [pltpu.VMEM((2, CORNER, width, TILE), f32)] * 4
         + [pltpu.VMEM((WIN * TILE, TILE_DEV * TILE), bf16)] * 2
+        + [pltpu.VMEM((TILE_DEV * TILE, WIN * TILE), bf16)] * 2
         + [pltpu.VMEM((WIN * width, WIN * TILE), bf16)] * 2
         + [pltpu.VMEM((len(HALO_SLOT), TILE, TILE), f32)]
+        + [pltpu.VMEM((len(OWN_SLOT), TILE, TILE), f32)]
         + [pltpu.SemaphoreType.DMA((2,))]
-        + [pltpu.SemaphoreType.DMA((24,))] * 2,
+        + [pltpu.SemaphoreType.DMA((18,))] * 2,
         compiler_params=pltpu.CompilerParams(
             collective_id=1, has_side_effects=True, vmem_limit_bytes=60 << 20
         ),

time: 92.1 us -> 85.3 us (0.926); the launches traced: 91.9 us -> 83.8 us
  Pallas kernels: 89.6 us -> 81.4 us
    pallas_call x1, Pallas kernels: 54.8 us -> 46.6 us  [local(): pl.pallas_call(functools.partial(band_kernel, rows, groups, scale), out_s...]
where the time goes in v4:
time: 85.3 us; the launch traced here: 83.8 us
  Pallas kernels  81.4 us (95%)
  local copies, waits for them, and re-layouts  2.36 us (3%)
    pallas_call x1, Pallas kernels, local(): pl.pallas_call(functools.partial(band_kernel, rows, groups, scale), out_s...  46.6 us
    pallas_call x1, Pallas kernels, local(): pl.pallas_call(functools.partial(route_kernel, rows, cap, groups), out_sh...  34.8 us
    unnamed x1, local copies, waits for them, and re-layouts  2.36 us

profile of v4, /device:TPU:9, one launch (start us, length us, event | category | flops | bytes accessed | tf_op | source)
XLA Modules:
  0.0 83.8 jit_solution(15733684585052381133)
XLA Ops:
  0.0 34.8 %shard_map.82 = (f32[72,32,128]{2,1,0:T(8,128)}, f32[72,32,128]{2,1,0:T(8,128)}) custom-call(bf16[256,256]{1,0:T(8,128)(2,1)} %feats_in.1, s32[1,256]{1,0:T(1,128)} %bitcast.4, s32[1,256]{1,0:T(1,128)} %bitcast.5, s32[1,256]{1,0:T(1,128)} %bitcast.6, s32[1,256]{1,0:T(1,128)} %bitcast.7, bf16[256,256]{1,0:T(8,128)(2,1)} %w1_in.1, bf16[256,256]{1,0:T(8,128)(2,1)} %w2_in.1, ...), custom_call_target="tpu_custom_call" | custom-call | tf_op jit(solution)/shard_map/pallas_call | solution.py:499
  34.8 46.6 %shard_map.83 = f32[8,9,32,128]{3,2,1,0:T(8,128)} custom-call(f32[72,32,128]{2,1,0:T(8,128)} %get-tuple-element.7.dh_in, f32[72,32,128]{2,1,0:T(8,128)} %get-tuple-element.8.rh_in), custom_call_target="tpu_custom_call" | custom-call | tf_op jit(solution)/shard_map/pallas_call | solution.py:520
  81.4 2.4 %copy.10 = f32[8,9,32,128]{3,2,1,0:T(8,128)} copy(f32[8,9,32,128]{3,2,1,0:T(8,128)} %shard_map.83) | data formatting | bytes 2359296

commit v5 on v4

--- a/solution.py
+++ b/solution.py
@@ -228,8 +228,8 @@
 
 
 def band_kernel(
-    rows, groups, scale, dh_in, rh_in, out,
-    dh, rh, le, lw, fe, fw, sp, rp, se, re, sw, rw, bhi, blo, fhi, flo, ahi, alo, t1, tw, sems, s_sem, r_sem,
+    rows, groups, scale, out,
+    dh, rh, le, lw, fe, fw, sp, rp, se, re, sw, rw, bhi, blo, fhi, flo, ahi, alo, t1, tw, s_sem, r_sem,
 ):
     r = lax.axis_index("rows")
     g = lax.axis_index("feat")
@@ -239,15 +239,6 @@
     core_peer, y_peer = y * 2 + (1 - c), (1 - y) * 2 + c
     mine = pl.ds(pl.multiple_of(g * width, width), width)
     theirs = pl.ds(pl.multiple_of(y_peer * width, width), width)
-
-    barrier = pltpu.get_barrier_semaphore()
-    for who in ((up, g), (down, g), (r, core_peer), (r, y_peer)):
-        pl.semaphore_signal(barrier, inc=1, device_id=who, device_id_type=MESH)
-
-    rh_fetch = pltpu.make_async_copy(rh_in, rh, sems.at[0])
-    dh_fetch = pltpu.make_async_copy(dh_in, dh, sems.at[1])
-    rh_fetch.start()
-    dh_fetch.start()
 
     def copy(src, dst, sem, who):
         return pltpu.make_async_remote_copy(
@@ -369,15 +360,12 @@
                 m = s + di
                 emit(2 * p + di, s, acc[m * width : (m + 1) * width, di * TILE : (di + 1) * TILE])
 
-    rh_fetch.wait()
     for n, (j, i) in enumerate(LOW_PART):
         sp[0, n] = rh[tile_at(j, i)]
     for n, (j, i) in enumerate(HIGH_PART):
         sp[1, n] = rh[tile_at(j, i)]
-    pl.semaphore_wait(barrier, 4)
     part_low = start(sp.at[0], rp.at[1], 0, (down, g))
     part_high = start(sp.at[1], rp.at[0], 1, (up, g))
-    dh_fetch.wait()
     for i, j in own_tiles():
         val = scale * (dh[tile_at(i, j)] + rh[tile_at(j, i)])
         le[tile_at(i, j)] = val
@@ -481,6 +469,13 @@
         item.wait_send()
 
 
+def whole_kernel(rows, cap, groups, scale, *refs):
+    operands, out, dh, rh = refs[:8], refs[8], refs[9], refs[10]
+    route_scratch, band_scratch = refs[11:26], refs[26:]
+    route_kernel(rows, cap, groups, *operands, dh, rh, *route_scratch)
+    band_kernel(rows, groups, scale, out, dh, rh, *band_scratch)
+
+
 def local(edge_feats, edge_owner, src_local, band_slot, dst_local, w_first, w_second, w_third):
     groups = lax.axis_size("feat")
     rows = lax.axis_size("rows")
@@ -496,12 +491,15 @@
     )
     partners = rows * groups
     sums = pltpu.VMEM((NT * NB, BLOCK // groups * TILE), f32)
-    by_col, by_row = pl.pallas_call(
-        functools.partial(route_kernel, rows, cap, groups),
-        out_shape=[jax.ShapeDtypeStruct(tiles, f32)] * 2,
+    degree = groups * edges / (TILE_DEV * NB)
+    scale = 0.5 * (0.5 / math.sqrt(2.0 * BLOCK * degree))
+    return pl.pallas_call(
+        functools.partial(whole_kernel, rows, cap, groups, scale),
+        out_shape=jax.ShapeDtypeStruct((TILE_DEV, BAND, width, TILE), f32),
         in_specs=[anywhere] * len(operands),
-        out_specs=[vm] * 2,
-        scratch_shapes=[pltpu.VMEM(item.shape, item.dtype) for item in operands]
+        out_specs=vm,
+        scratch_shapes=[pltpu.VMEM(tiles, f32)] * 2
+        + [pltpu.VMEM(item.shape, item.dtype) for item in operands]
         + [
             pltpu.VMEM((rows, groups, cap, LANES), f32),
             pltpu.VMEM((partners, cap, LANES), f32),
@@ -510,19 +508,8 @@
             pltpu.SemaphoreType.DMA((len(operands),)),
             pltpu.SemaphoreType.DMA((partners,)),
             pltpu.SemaphoreType.DMA((partners,)),
-        ],
-        compiler_params=pltpu.CompilerParams(
-            collective_id=0, has_side_effects=True, vmem_limit_bytes=56 << 20
-        ),
-    )(*operands)
-    degree = groups * edges / (TILE_DEV * NB)
-    scale = 0.5 * (0.5 / math.sqrt(2.0 * BLOCK * degree))
-    return pl.pallas_call(
-        functools.partial(band_kernel, rows, groups, scale),
-        out_shape=jax.ShapeDtypeStruct((TILE_DEV, BAND, width, TILE), f32),
-        in_specs=[anywhere] * 2,
-        out_specs=vm,
-        scratch_shapes=[pltpu.VMEM(tiles, f32)] * 4
+        ]
+        + [pltpu.VMEM(tiles, f32)] * 2
         + [pltpu.VMEM((SENT, TILE, TILE), f32)] * 2
         + [pltpu.VMEM((2, PART, width, TILE), f32)] * 2
         + [pltpu.VMEM((2, CORNER, width, TILE), f32)] * 4
@@ -531,12 +518,11 @@
         + [pltpu.VMEM((WIN * width, WIN * TILE), bf16)] * 2
         + [pltpu.VMEM((len(HALO_SLOT), TILE, TILE), f32)]
         + [pltpu.VMEM((len(OWN_SLOT), TILE, TILE), f32)]
-        + [pltpu.SemaphoreType.DMA((2,))]
         + [pltpu.SemaphoreType.DMA((18,))] * 2,
         compiler_params=pltpu.CompilerParams(
-            collective_id=1, has_side_effects=True, vmem_limit_bytes=60 << 20
+            collective_id=0, has_side_effects=True, vmem_limit_bytes=60 << 20
         ),
-    )(by_col, by_row)
+    )(*operands)
 
 
 def solution(mesh):

time: 85.3 us -> 80.6 us (0.945)
  Pallas kernels: 81.4 us -> 76.9 us
    pallas_call x2 -> x1, Pallas kernels: 81.4 us -> 76.9 us  [local(): pl.pallas_call(functools.partial(whole_kernel, rows, cap, groups, scale),...]
where the time goes in v5:
time: 80.6 us; the launch traced here: 79.3 us
  Pallas kernels  76.9 us (95%)
  local copies, waits for them, and re-layouts  2.36 us (3%)
    pallas_call x1, Pallas kernels, local(): pl.pallas_call(functools.partial(whole_kernel, rows, cap, groups, scale),...  76.9 us
    unnamed x1, local copies, waits for them, and re-layouts  2.36 us

profile of v5, /device:TPU:9, one launch (start us, length us, event | category | flops | bytes accessed | tf_op | source)
XLA Modules:
  0.0 79.3 jit_solution(2398650797332150084)
XLA Ops:
  0.0 76.9 %shard_map.82 = f32[8,9,32,128]{3,2,1,0:T(8,128)} custom-call(bf16[256,256]{1,0:T(8,128)(2,1)} %refs_0_.1, s32[1,256]{1,0:T(1,128)} %bitcast.4, s32[1,256]{1,0:T(1,128)} %bitcast.5, s32[1,256]{1,0:T(1,128)} %bitcast.6, s32[1,256]{1,0:T(1,128)} %bitcast.7, bf16[256,256]{1,0:T(8,128)(2,1)} %refs_5_.1, bf16[256,256]{1,0:T(8,128)(2,1)} %refs_6_.1, ...), custom_call_target="tpu_custom_call" | custom-call | tf_op jit(solution)/shard_map/pallas_call | solution.py:496
  76.9 2.4 %copy.10 = f32[8,9,32,128]{3,2,1,0:T(8,128)} copy(f32[8,9,32,128]{3,2,1,0:T(8,128)} %shard_map.82) | data formatting | bytes 2359296

commit v6 on v5

--- a/solution.py
+++ b/solution.py
@@ -350,15 +350,25 @@
             lw[tile_at(i, j)] = val
             fw[E_AT[i, j], mine, :] = val
 
-    def product(p, emit):
-        rows_at = slice(2 * p * width, (2 * p + 10) * width)
+    def product(p, emit, inside):
+        first, last = 2 * p, 2 * p + 10
+        if inside:
+            first, last = max(first, HALF), min(last, HALF + TILE_DEV)
+        elif p < PAIRS // 2:
+            last = HALF
+        else:
+            first = HALF + TILE_DEV
         mid = slice(2 * p * TILE, (2 * p + 10) * TILE)
         cols_at = slice(2 * p * TILE, (2 * p + 2) * TILE)
-        acc = three((ahi, alo), (rows_at, mid), right, (mid, cols_at))
+        acc = three((ahi, alo), (slice(first * width, last * width), mid), right, (mid, cols_at))
         for di in range(2):
             for s in range(BAND):
-                m = s + di
-                emit(2 * p + di, s, acc[m * width : (m + 1) * width, di * TILE : (di + 1) * TILE])
+                m = 2 * p + di + s - first
+                if 0 <= m < last - first:
+                    emit(
+                        2 * p + di, s,
+                        acc[m * width : (m + 1) * width, di * TILE : (di + 1) * TILE],
+                    )
 
     for n, (j, i) in enumerate(LOW_PART):
         sp[0, n] = rh[tile_at(j, i)]
@@ -434,13 +444,13 @@
     corners[0] = start(sw.at[1], rw.at[0], 14, (up, g))
     own_parts([t for t in E_CHUNKS[0] if t[0] < HALF <= t[1]])
 
-    chunks = []
+    chunks = [None, None]
     halos = (to_high, to_low)
-    for side in range(2):
+    for side in (1, 0):
         halos[side].wait_recv()
         build_corner(re, side)
         halo_side(side)
-        chunks.append(gather(fw, OWN + side * SIDE, SIDE, (10, 15)[side]))
+        chunks[side] = gather(fw, OWN + side * SIDE, SIDE, (10, 15)[side])
     build_own_square()
     for i in range(TILE_DEV):
         for s in range(BAND):
@@ -456,15 +466,18 @@
             val = val + 0.4375 * eye
         out[i, s] = val
 
-    for half in range(2):
+    for half in (1, 0):
         on = forward(chunks[half])
         chunks[half][0].wait_recv()
         on.wait_recv()
         build_side(SIDES[half])
+        for p in (2 * half, 2 * half + 1):
+            product(p, second, True)
+    for half in (1, 0):
         corners[half].wait_recv()
         build_corner(rw, half)
         for p in (2 * half, 2 * half + 1):
-            product(p, second)
+            product(p, second, False)
     for item in pending:
         item.wait_send()
 

time: 80.6 us -> 81.2 us (level)
    pallas_call x1, Pallas kernels: 76.9 us -> 77.7 us  [local(): pl.pallas_call(functools.partial(whole_kernel, rows, cap, groups, scale),...]
where the time goes in v6:
time: 81.2 us; the launch traced here: 80.1 us
  Pallas kernels  77.7 us (96%)
  local copies, waits for them, and re-layouts  2.36 us (3%)
    pallas_call x1, Pallas kernels, local(): pl.pallas_call(functools.partial(whole_kernel, rows, cap, groups, scale),...  77.7 us
    unnamed x1, local copies, waits for them, and re-layouts  2.36 us

profile of v6, /device:TPU:9, one launch (start us, length us, event | category | flops | bytes accessed | tf_op | source)
XLA Modules:
  0.0 80.1 jit_solution(134615435731666484)
XLA Ops:
  0.0 77.7 %shard_map.82 = f32[8,9,32,128]{3,2,1,0:T(8,128)} custom-call(bf16[256,256]{1,0:T(8,128)(2,1)} %refs_0_.1, s32[1,256]{1,0:T(1,128)} %bitcast.4, s32[1,256]{1,0:T(1,128)} %bitcast.5, s32[1,256]{1,0:T(1,128)} %bitcast.6, s32[1,256]{1,0:T(1,128)} %bitcast.7, bf16[256,256]{1,0:T(8,128)(2,1)} %refs_5_.1, bf16[256,256]{1,0:T(8,128)(2,1)} %refs_6_.1, ...), custom_call_target="tpu_custom_call" | custom-call | tf_op jit(solution)/shard_map/pallas_call | solution.py:509
  77.7 2.4 %copy.10 = f32[8,9,32,128]{3,2,1,0:T(8,128)} copy(f32[8,9,32,128]{3,2,1,0:T(8,128)} %shard_map.82) | data formatting | bytes 2359296
